TPU v7x, 256 devices: a whole 4x4x8 slice. The times are simulated.
256 devices in a mesh: inter: 8 (over x, y_lo), intra: 32 (over y_hi, z, core).
Axes of the slice: x: 4, y: 4 (y_hi: 2, y_lo: 2; y = y_hi * 2 + y_lo), z: 8, core: 2. Of those that a mesh axis runs over, the one named last changes fastest.
Arguments:
- grads: bfloat16 [256, 4194304], P(('inter', 'intra')), may hold values from -16 to 16
- params: float32 [4194304], P(('inter', 'intra')), may hold values from -6 to 6
- moment_one: float32 [4194304], P(('inter', 'intra')), may hold values from -6 to 6
- moment_two: float32 [4194304], P(('inter', 'intra')), may hold values from 0.1 to 2
Outputs:
- new_params: float32 [4194304], P(('inter', 'intra'))
- new_moment_one: float32 [4194304], P(('inter', 'intra'))
- new_moment_two: float32 [4194304], P(('inter', 'intra'))
All inputs are finite; a program needn't handle non-finite values.
Results may differ from a plain program's by a relative error of at most 0.0003.
Values may be sent and summed in bfloat16 or wider, within the bound.
No kernel may reach another device: no remote copies, remote signals or barrier semaphores. Data moves between devices by JAX's collectives and lax.ppermute only.
A program may use at most 128 MiB of HBM per device.

v0:
```python
import jax
import jax.numpy as jnp
from jax import lax
from jax.sharding import PartitionSpec as P

SHARD = 16384


def add_sources(arrived):
    return jnp.sum(arrived.astype(jnp.float32), axis=1)


def per_device(grads, params, moment_one, moment_two):
    n_inter = lax.axis_size("inter")
    n_intra = lax.axis_size("intra")
    shaped = grads.reshape(n_inter, n_intra, SHARD)
    group_sum = add_sources(
        lax.all_to_all(shaped, "intra", split_axis=1, concat_axis=1, tiled=True)
    )
    sums_all = lax.all_to_all(group_sum, "inter", split_axis=0, concat_axis=0, tiled=True)
    summed = jnp.sum(sums_all, axis=0)
    new_one = 0.9 * moment_one + 0.1 * summed
    new_two = 0.999 * moment_two + 0.001 * summed * summed
    update = new_one / (1.0 - 0.9**10) / (jnp.sqrt(new_two / (1.0 - 0.999**10)) + 1e-08)
    return (params - 0.1 * update, new_one, new_two)


def solution(mesh):
    in_specs = (
        P(("inter", "intra"), None),
        P(("inter", "intra")),
        P(("inter", "intra")),
        P(("inter", "intra")),
    )
    out_specs = (P(("inter", "intra")), P(("inter", "intra")), P(("inter", "intra")))
    return jax.shard_map(
        per_device, mesh=mesh, in_specs=in_specs, out_specs=out_specs, check_vma=False
    )
```

profile of v0, /device:TPU:16, one launch (start us, length us, event | category | flops | bytes accessed | tf_op | source)
XLA Modules:
  0.0 416.5 jit_solution(10602708730216473776)
XLA Ops:
  0.6 178.3 %reduce.1 = bf16[4194304]{0:T(1024)(128)(2,1)} reduce(bf16[1,4194304]{1,0:T(2,128)(2,1)} %param.4, bf16[]{:T(256)} %constant.19), dimensions={0}, to_apply=%param.4.reduce_sub_computation | reduce | bytes 16777218 | tf_op args[0]
  178.9 13.3 %reshape.11 = bf16[8,32,16384]{2,1,0:T(8,128)(2,1)} reshape(bf16[4194304]{0:T(1024)(128)(2,1)} %reduce.1) | data formatting | bytes 16777216 | tf_op jit(solution)/shard_map/reshape | solution.py:16
  192.2 11.2 %copy.7 = bf16[8,32,16384]{2,0,1:T(8,128)(2,1)} copy(bf16[8,32,16384]{2,1,0:T(8,128)(2,1)} %reshape.11) | data formatting | bytes 16777216 | tf_op jit(solution)/shard_map/reshape | solution.py:16
  203.4 196.1 %all_to_all.14 = bf16[8,32,16384]{2,0,1:T(8,128)(2,1)S(1)} all-to-all(bf16[8,32,16384]{2,0,1:T(8,128)(2,1)} %copy.7), channel_id=1, replica_groups=mesh['inter'=8,'intra'=32] {'intra'}, dimensions={1} | all-to-all | bytes 16777216 | tf_op jit(solution)/shard_map/all_to_all | solution.py:18
  399.6 0.0 copy-start
  399.6 0.0 copy-start.1
  399.6 0.0 copy-start.2
  399.6 1.3 convert_reduce_fusion
  400.9 0.4 all_to_all.10
  401.2 14.1 %all_to_all.15 = f32[8,1,16384]{2,1,0:T(1,128)S(1)} all-to-all(f32[8,1,16384]{2,1,0:T(1,128)S(1)} %all_to_all.10), channel_id=1, replica_groups=mesh['inter'=8,'intra'=32] {'inter'}, dimensions={0} | all-to-all | bytes 1048576 | tf_op jit(solution)/shard_map/all_to_all | solution.py:20
  415.3 0.4 reduce_sum.19
  415.7 0.0 copy-done
  415.7 0.0 copy-done.1
  415.8 0.0 copy-done.2
  415.8 0.7 multiply_subtract_fusion
Async XLA Ops:
  399.6 16.2 %copy-start = (f32[16384]{0:T(1024)S(1)}, f32[16384]{0:T(1024)}, u32[]{:S(2)}) copy-start(f32[16384]{0:T(1024)} %param.5) | copy-start | bytes 196612
  399.6 16.2 %copy-start.1 = (f32[16384]{0:T(1024)S(1)}, f32[16384]{0:T(1024)}, u32[]{:S(2)}) copy-start(f32[16384]{0:T(1024)} %param.6) | copy-start | bytes 196612
  399.6 16.2 %copy-start.2 = (f32[16384]{0:T(1024)S(1)}, f32[16384]{0:T(1024)}, u32[]{:S(2)}) copy-start(f32[16384]{0:T(1024)} %param.7) | copy-start | bytes 196612
where the time goes:
time: 419 us; the launch traced here: 416 us
  blocking collectives  210 us (50%)
  other arithmetic  181 us (43%)
  local copies, waits for them, and re-layouts  24.9 us (6%)
    all_to_all x1, blocking collectives, per_device(): lax.all_to_all(shaped, 'intra', split_axis=1, concat_axis=1, tiled=True)  196 us
    unnamed x1, other arithmetic  178 us
    reshape x2, local copies, waits for them, and re-layouts, per_device(): shaped = grads.reshape(n_inter, n_intra, SHARD)  24.5 us
    all_to_all x1, blocking collectives, per_device(): lax.all_to_all(group_sum, 'inter', split_axis=0, concat_axis=0, tiled=True)  14.1 us

commit v1 on v0

v1 whole, which is shorter than its diff:
```python
import functools

import jax
import jax.numpy as jnp
from jax import lax
from jax.experimental import pallas as pl
from jax.experimental.pallas import tpu as pltpu
from jax.sharding import Mesh, PartitionSpec as P

SHARD = 16384
LANES = 128
ROWS = SHARD // LANES
NX, NYL, NYH, NZ, NCORE = 4, 2, 2, 8, 2
NY = NYL * NYH
AXES = ("x", "ylo", "yhi", "z", "core")
GROUP = NZ * SHARD
SCALE = 1024.0
CHUNKS = ((2, 1), (3, 0))


def device_index(x, y, z, core):
    return (((x * NYL + y % NYL) * NYH + y // NYL) * NZ + z) * NCORE + core


def permutation(offset, stage):
    pairs = []
    for x in range(NX):
        for y in range(NY):
            for z in range(NZ):
                for core in range(NCORE):
                    if core == stage:
                        to = device_index((x + offset) % NX, y, z, core)
                    else:
                        to = device_index(x, (y + offset) % NY, z, core)
                    pairs.append((device_index(x, y, z, core), to))
    return pairs


SWAP = [(d, d ^ 1) for d in range(NX * NY * NZ * NCORE)]


def repack_kernel(chunk, grads, send, keep, raw, packed, in_sem, out_sem):
    n = len(chunk)
    x = lax.axis_index("x")
    y = lax.axis_index("yhi") * NYL + lax.axis_index("ylo")
    core = lax.axis_index("core")
    groups = [
        (half, first, j) for half in range(2) for j in range(n) for first in range(4)
    ]

    def start(g, half, first, second):
        owner = 1 - core if half == 0 else core
        dx = jnp.where(owner == 0, first, second)
        dy = jnp.where(owner == 0, second, first)
        gx = lax.rem(x + dx, NX)
        gy = lax.rem(y + dy, NY)
        base = ((gx * NYL + lax.rem(gy, NYL)) * NYH + gy // NYL) * (NZ * NCORE) + owner

        def one(z, carry):
            pltpu.make_async_copy(
                grads.at[:, pl.ds(pl.multiple_of((base + z * NCORE) * SHARD, SHARD), SHARD)],
                raw.at[:, pl.ds(pl.multiple_of(g * GROUP + z * SHARD, SHARD), SHARD)],
                in_sem.at[g],
            ).start()
            return carry

        lax.fori_loop(0, NZ, one, 0)

    for g, (half, first, j) in enumerate(groups):
        start(g, half, first, chunk[j])
    outs = []
    for g, (half, first, j) in enumerate(groups):
        pltpu.make_async_copy(
            grads.at[:, pl.ds(0, GROUP)], raw.at[:, pl.ds(g * GROUP, GROUP)], in_sem.at[g]
        ).wait()

        def one(z, carry):
            at = pl.multiple_of(g * GROUP + z * SHARD, SHARD)
            packed[g, z] = raw[:, pl.ds(at, SHARD)].reshape(ROWS, LANES)
            return carry

        lax.fori_loop(0, NZ, one, 0)
        out = pltpu.make_async_copy(
            packed.at[g], (send, keep)[half].at[first, j], out_sem.at[g]
        )
        out.start()
        outs.append(out)
    for out in outs:
        out.wait()


def repack(grads, chunk):
    n = len(chunk)
    shape = jax.ShapeDtypeStruct((4, n, NZ, ROWS, LANES), jnp.bfloat16)
    return pl.pallas_call(
        functools.partial(repack_kernel, chunk),
        out_shape=(shape, shape),
        in_specs=[pl.BlockSpec(memory_space=pl.ANY)],
        out_specs=(pl.BlockSpec(memory_space=pl.ANY),) * 2,
        scratch_shapes=[
            pltpu.VMEM((1, 8 * n * GROUP), jnp.bfloat16),
            pltpu.VMEM((8 * n, NZ, ROWS, LANES), jnp.bfloat16),
            pltpu.SemaphoreType.DMA((8 * n,)),
            pltpu.SemaphoreType.DMA((8 * n,)),
        ],
        compiler_params=pltpu.CompilerParams(vmem_limit_bytes=48 << 20),
        cost_estimate=pl.CostEstimate(
            flops=0, bytes_accessed=8 * n * GROUP * 6, transcendentals=0
        ),
    )(grads)


def encode(value):
    return (value * SCALE).astype(jnp.float16)


def decode(value):
    return value.astype(jnp.float32) * (1.0 / SCALE)


def first_stage(grads, chunk):
    send, keep = repack(grads, chunk)
    got = lax.ppermute(send, AXES, SWAP)

    def pair(k):
        return keep[k].astype(jnp.float32) + got[k].astype(jnp.float32)

    total = pair(0)
    for k in (2, 1, 3):
        total = total + decode(lax.ppermute(encode(pair(k)), AXES, permutation(k, 0)))
    return {q: total[j] for j, q in enumerate(chunk)}


def per_device(grads, params, moment_one, moment_two):
    parts = {}
    for chunk in CHUNKS:
        parts.update(first_stage(grads, chunk))
    total = parts[0]
    for k in (2, 1, 3):
        total = total + lax.ppermute(parts[k], AXES, permutation(k, 1))
    arrived = lax.all_to_all(total, "z", split_axis=0, concat_axis=0, tiled=True)
    summed = jnp.sum(arrived, axis=0).reshape(SHARD)
    new_one = 0.9 * moment_one + 0.1 * summed
    new_two = 0.999 * moment_two + 0.001 * summed * summed
    update = new_one / (1.0 - 0.9**10) / (jnp.sqrt(new_two / (1.0 - 0.999**10)) + 1e-08)
    return (params - 0.1 * update, new_one, new_two)


def solution(mesh):
    split = Mesh(mesh.devices.reshape(NX, NYL, NYH, NZ, NCORE), AXES)
    in_specs = (P(AXES, None), P(AXES), P(AXES), P(AXES))
    out_specs = (P(AXES), P(AXES), P(AXES))
    return jax.shard_map(
        per_device, mesh=split, in_specs=in_specs, out_specs=out_specs, check_vma=False
    )
```

time: 419 us -> 90.3 us (0.22)
  blocking collectives: 210 us -> 24.6 us
  other arithmetic: 181 us -> 3.04 us
  waiting for transfers between devices: 0 us -> 33.6 us
  local copies, waits for them, and re-layouts: 24.9 us -> 0.14 us
  Pallas kernels: 0 us -> 14.3 us
  starting transfers between devices: 0 us -> 13.6 us
    all_to_all x2 -> x1, blocking collectives: 210 us -> 24.6 us  [per_device(): lax.all_to_all(total, 'z', split_axis=0, concat_axis=0, tiled=True)]
    unnamed x1 -> x0, other arithmetic: 178 us -> none
    ppermute x0 -> x11, waiting for transfers between devices: none -> 33.6 us  [the longest x6 24.9 us: first_stage(): lax.ppermute(encode(pair(k)), AXES, permutation(k, 0))]
    reshape x2 -> x0, local copies, waits for them, and re-layouts: 24.5 us -> none  [per_device(): shaped = grads.reshape(n_inter, n_intra, SHARD)]
    pallas_call x0 -> x2, Pallas kernels: none -> 14.3 us  [repack(): pl.pallas_call(functools.partial(repack_kernel, chunk), out_shape=(shape,...]
    ppermute x0 -> x11, starting transfers between devices: none -> 13.6 us  [the longest x6 9.98 us: first_stage(): lax.ppermute(encode(pair(k)), AXES, permutation(k, 0))]
  transfers between devices with their start and end apart: 0 -> 11, of which waited for: 0 -> 6; matrix products, arithmetic and copies ran while one was open for 0% -> 3% of each run, Pallas kernels for 0% -> 8%
where the time goes in v1:
time: 90.3 us; the launch traced here: 90.2 us
  waiting for transfers between devices  33.6 us (37%)
  blocking collectives  24.6 us (27%)
  Pallas kernels  14.3 us (16%)
  starting transfers between devices  13.6 us (15%)
  other arithmetic  3.04 us (3%)
    ppermute x6, waiting for transfers between devices, first_stage(): lax.ppermute(encode(pair(k)), AXES, permutation(k, 0))  24.9 us
    all_to_all x1, blocking collectives, per_device(): lax.all_to_all(total, 'z', split_axis=0, concat_axis=0, tiled=True)  24.6 us
    pallas_call x2, Pallas kernels, repack(): pl.pallas_call(functools.partial(repack_kernel, chunk), out_shape=(shape,...  14.3 us
    ppermute x6, starting transfers between devices, first_stage(): lax.ppermute(encode(pair(k)), AXES, permutation(k, 0))  9.98 us
    ppermute x3, waiting for transfers between devices, per_device(): total = total + lax.ppermute(parts[k], AXES, permutation(k, 1))  8.73 us
    ppermute x3, starting transfers between devices, per_device(): total = total + lax.ppermute(parts[k], AXES, permutation(k, 1))  3.13 us
  transfers between devices with their start and end apart: 11, of which 6 were waited for; matrix products, arithmetic and copies ran while one was open for 3% of the time, Pallas kernels for 8%

profile of v1, /device:TPU:16, one launch (start us, length us, event | category | flops | bytes accessed | tf_op | source)
XLA Modules:
  0.0 90.2 jit_solution(3550656175734595709)
XLA Ops:
  0.6 7.2 %shard_map.68 = (bf16[4,2,8,128,128]{4,3,2,1,0:T(8,128)(2,1)S(1)}, bf16[4,2,8,128,128]{4,3,2,1,0:T(8,128)(2,1)S(1)}) custom-call(bf16[1,4194304]{1,0:T(2,128)(2,1)} %grads.3), custom_call_target="tpu_custom_call" | custom-call | bytes 12582912 | tf_op jit(solution)/shard_map/pallas_call | solution.py:95
  7.8 0.1 collective-permute-start.4
  7.9 7.2 %shard_map.67 = (bf16[4,2,8,128,128]{4,3,2,1,0:T(8,128)(2,1)S(1)}, bf16[4,2,8,128,128]{4,3,2,1,0:T(8,128)(2,1)S(1)}) custom-call(bf16[1,4194304]{1,0:T(2,128)(2,1)} %grads.3), custom_call_target="tpu_custom_call" | custom-call | bytes 12582912 | tf_op jit(solution)/shard_map/pallas_call | solution.py:95
  15.1 0.4 collective-permute-start
  15.5 0.0 collective-permute-done.4
  15.5 0.6 fusion.7
  16.2 3.1 %collective-permute-start.5 = (f16[2,8,128,128]{3,2,1,0:T(8,128)(2,1)S(1)}, f16[2,8,128,128]{3,2,1,0:T(8,128)(2,1)S(1)}, u32[]{:S(2)}, u32[]{:S(2)}) collective-permute-start(f16[2,8,128,128]{3,2,1,0:T(8,128)(2,1)S(1)} %get-tuple-element.14), channel_id=1, source_target_pairs={{0,128},{1,17},{2,130},{3,19},{4,132},{5,21},{6,134},{7,23},{8,136... | collective-permute-start | bytes 1572872 | tf_op jit(solution)/shard_map/ppermute | solution.py:130
  19.3 1.1 %collective-permute-start.7 = (f16[2,8,128,128]{3,2,1,0:T(8,128)(2,1)S(1)}, f16[2,8,128,128]{3,2,1,0:T(8,128)(2,1)S(1)}, u32[]{:S(2)}, u32[]{:S(2)}) collective-permute-start(f16[2,8,128,128]{3,2,1,0:T(8,128)(2,1)S(1)} %get-tuple-element.15), channel_id=1, source_target_pairs={{0,192},{1,49},{2,194},{3,51},{4,196},{5,53},{6,198},{7,55},{8,200... | collective-permute-start | bytes 1572872 | tf_op jit(solution)/shard_map/ppermute | solution.py:130
  20.4 0.9 collective-permute-start.6
  21.3 0.0 collective-permute-done
  21.3 0.6 fusion.4
  21.9 1.2 %collective-permute-start.1 = (f16[2,8,128,128]{3,2,1,0:T(8,128)(2,1)S(1)}, f16[2,8,128,128]{3,2,1,0:T(8,128)(2,1)S(1)}, u32[]{:S(2)}, u32[]{:S(2)}) collective-permute-start(f16[2,8,128,128]{3,2,1,0:T(8,128)(2,1)S(1)} %get-tuple-element.17), channel_id=1, source_target_pairs={{0,128},{1,17},{2,130},{3,19},{4,132},{5,21},{6,134},{7,23},{8,136... | collective-permute-start | bytes 1572872 | tf_op jit(solution)/shard_map/ppermute | solution.py:130
  23.1 2.2 %collective-permute-start.3 = (f16[2,8,128,128]{3,2,1,0:T(8,128)(2,1)S(1)}, f16[2,8,128,128]{3,2,1,0:T(8,128)(2,1)S(1)}, u32[]{:S(2)}, u32[]{:S(2)}) collective-permute-start(f16[2,8,128,128]{3,2,1,0:T(8,128)(2,1)S(1)} %get-tuple-element.18), channel_id=1, source_target_pairs={{0,192},{1,49},{2,194},{3,51},{4,196},{5,53},{6,198},{7,55},{8,200... | collective-permute-start | bytes 1572872 | tf_op jit(solution)/shard_map/ppermute | solution.py:130
  25.3 1.8 %collective-permute-done.5 = f16[2,8,128,128]{3,2,1,0:T(8,128)(2,1)S(1)} collective-permute-done((f16[2,8,128,128]{3,2,1,0:T(8,128)(2,1)S(1)}, f16[2,8,128,128]{3,2,1,0:T(8,128)(2,1)S(1)}, u32[]{:S(2)}, u32[]{:S(2)}) %collective-permute-start.5) | collective-permute-done | bytes 524320 | tf_op jit(solution)/shard_map/ppermute | solution.py:130
  27.0 1.5 %collective-permute-start.2 = (f16[2,8,128,128]{3,2,1,0:T(8,128)(2,1)S(1)}, f16[2,8,128,128]{3,2,1,0:T(8,128)(2,1)S(1)}, u32[]{:S(2)}, u32[]{:S(2)}) collective-permute-start(f16[2,8,128,128]{3,2,1,0:T(8,128)(2,1)S(1)} %get-tuple-element.19), channel_id=1, source_target_pairs={{0,64},{1,33},{2,66},{3,35},{4,68},{5,37},{6,70},{7,39},{8,72},{9,... | collective-permute-start | bytes 1572872 | tf_op jit(solution)/shard_map/ppermute | solution.py:130
  28.5 4.2 %collective-permute-done.7 = f16[2,8,128,128]{3,2,1,0:T(8,128)(2,1)S(1)} collective-permute-done((f16[2,8,128,128]{3,2,1,0:T(8,128)(2,1)S(1)}, f16[2,8,128,128]{3,2,1,0:T(8,128)(2,1)S(1)}, u32[]{:S(2)}, u32[]{:S(2)}) %collective-permute-start.7) | collective-permute-done | bytes 524320 | tf_op jit(solution)/shard_map/ppermute | solution.py:130
  32.7 0.0 collective-permute-done.6
  32.7 0.5 fusion.1
  33.2 0.1 slice_bitcast_fusion.2
  33.3 2.0 %collective-permute-start.8 = (f32[8,128,128]{2,1,0:T(8,128)S(1)}, f32[8,128,128]{2,1,0:T(8,128)S(1)}, u32[]{:S(2)}, u32[]{:S(2)}) collective-permute-start(f32[8,128,128]{2,1,0:T(8,128)S(1)} %get-tuple-element.20), channel_id=1, source_target_pairs={{0,16},{1,129},{2,18},{3,131},{4,20},{5,133},{6,22},{7,135},{8,24}... | collective-permute-start | bytes 1572872 | tf_op jit(solution)/shard_map/ppermute | solution.py:140
  35.3 0.6 collective-permute-start.9
  35.9 4.0 %collective-permute-done.1 = f16[2,8,128,128]{3,2,1,0:T(8,128)(2,1)S(1)} collective-permute-done((f16[2,8,128,128]{3,2,1,0:T(8,128)(2,1)S(1)}, f16[2,8,128,128]{3,2,1,0:T(8,128)(2,1)S(1)}, u32[]{:S(2)}, u32[]{:S(2)}) %collective-permute-start.1) | collective-permute-done | bytes 524320 | tf_op jit(solution)/shard_map/ppermute | solution.py:130
  39.8 9.7 %collective-permute-done.3 = f16[2,8,128,128]{3,2,1,0:T(8,128)(2,1)S(1)} collective-permute-done((f16[2,8,128,128]{3,2,1,0:T(8,128)(2,1)S(1)}, f16[2,8,128,128]{3,2,1,0:T(8,128)(2,1)S(1)}, u32[]{:S(2)}, u32[]{:S(2)}) %collective-permute-start.3) | collective-permute-done | bytes 524320 | tf_op jit(solution)/shard_map/ppermute | solution.py:130
  49.6 5.3 %collective-permute-done.2 = f16[2,8,128,128]{3,2,1,0:T(8,128)(2,1)S(1)} collective-permute-done((f16[2,8,128,128]{3,2,1,0:T(8,128)(2,1)S(1)}, f16[2,8,128,128]{3,2,1,0:T(8,128)(2,1)S(1)}, u32[]{:S(2)}, u32[]{:S(2)}) %collective-permute-start.2) | collective-permute-done | bytes 524320 | tf_op jit(solution)/shard_map/ppermute | solution.py:130
  54.8 0.5 fusion.3
  55.3 0.0 copy-start
  55.4 0.0 copy-start.1
  55.4 0.0 copy-start.2
  55.4 0.5 collective-permute-start.10
  55.9 0.0 collective-permute-done.8
  55.9 0.0 collective-permute-done.9
  55.9 8.7 %collective-permute-done.10 = f32[8,128,128]{2,1,0:T(8,128)S(1)} collective-permute-done((f32[8,128,128]{2,1,0:T(8,128)S(1)}, f32[8,128,128]{2,1,0:T(8,128)S(1)}, u32[]{:S(2)}, u32[]{:S(2)}) %collective-permute-start.10) | collective-permute-done | bytes 524320 | tf_op jit(solution)/shard_map/ppermute | solution.py:140
  64.6 0.1 fusion.12
  64.8 24.6 %all_to_all.5 = f32[8,128,128]{2,1,0:T(8,128)S(1)} all-to-all(f32[8,128,128]{2,1,0:T(8,128)S(1)} %fusion.12), channel_id=1, replica_groups=mesh['x'=4,'ylo'=2,'yhi'=2,'z'=8,'core'=2] {'z'}, dimensions={0} | all-to-all | bytes 1048576 | tf_op jit(solution)/shard_map/all_to_all | solution.py:141
  89.4 0.0 copy-done
  89.5 0.0 copy-done.1
  89.5 0.0 copy-done.2
  89.5 0.7 multiply_subtract_fusion
  (2 shorter events, 0.1 us)
Async XLA Ops:
  7.8 7.7 %collective-permute-start.4 = (bf16[4,2,8,128,128]{4,3,2,1,0:T(8,128)(2,1)S(1)}, bf16[4,2,8,128,128]{4,3,2,1,0:T(8,128)(2,1)S(1)}, u32[]{:S(2)}, u32[]{:S(2)}) collective-permute-start(bf16[4,2,8,128,128]{4,3,2,1,0:T(8,128)(2,1)S(1)} %get-tuple-element.10), channel_id=1, source_target_pairs={{0,1},{1,0},{2,3},{3,2},{4,5},{5,4},{6,7},{7,6},{8,9},{9,8},{10,11... | collective-permute-start | bytes 6291464 | tf_op jit(solution)/shard_map/ppermute | solution.py:123
  15.1 6.2 %collective-permute-start = (bf16[4,2,8,128,128]{4,3,2,1,0:T(8,128)(2,1)S(1)}, bf16[4,2,8,128,128]{4,3,2,1,0:T(8,128)(2,1)S(1)}, u32[]{:S(2)}, u32[]{:S(2)}) collective-permute-start(bf16[4,2,8,128,128]{4,3,2,1,0:T(8,128)(2,1)S(1)} %get-tuple-element.8), channel_id=1, source_target_pairs={{0,1},{1,0},{2,3},{3,2},{4,5},{5,4},{6,7},{7,6},{8,9},{9,8},{10,11... | collective-permute-start | bytes 6291464 | tf_op jit(solution)/shard_map/ppermute | solution.py:123
  16.2 10.9 %collective-permute-start.5 = (f16[2,8,128,128]{3,2,1,0:T(8,128)(2,1)S(1)}, f16[2,8,128,128]{3,2,1,0:T(8,128)(2,1)S(1)}, u32[]{:S(2)}, u32[]{:S(2)}) collective-permute-start(f16[2,8,128,128]{3,2,1,0:T(8,128)(2,1)S(1)} %get-tuple-element.14), channel_id=1, source_target_pairs={{0,128},{1,17},{2,130},{3,19},{4,132},{5,21},{6,134},{7,23},{8,136... | collective-permute-start | bytes 1572872 | tf_op jit(solution)/shard_map/ppermute | solution.py:130
  19.3 13.4 %collective-permute-start.7 = (f16[2,8,128,128]{3,2,1,0:T(8,128)(2,1)S(1)}, f16[2,8,128,128]{3,2,1,0:T(8,128)(2,1)S(1)}, u32[]{:S(2)}, u32[]{:S(2)}) collective-permute-start(f16[2,8,128,128]{3,2,1,0:T(8,128)(2,1)S(1)} %get-tuple-element.15), channel_id=1, source_target_pairs={{0,192},{1,49},{2,194},{3,51},{4,196},{5,53},{6,198},{7,55},{8,200... | collective-permute-start | bytes 1572872 | tf_op jit(solution)/shard_map/ppermute | solution.py:130
  20.4 12.3 %collective-permute-start.6 = (f16[2,8,128,128]{3,2,1,0:T(8,128)(2,1)S(1)}, f16[2,8,128,128]{3,2,1,0:T(8,128)(2,1)S(1)}, u32[]{:S(2)}, u32[]{:S(2)}) collective-permute-start(f16[2,8,128,128]{3,2,1,0:T(8,128)(2,1)S(1)} %get-tuple-element.16), channel_id=1, source_target_pairs={{0,64},{1,33},{2,66},{3,35},{4,68},{5,37},{6,70},{7,39},{8,72},{9,... | collective-permute-start | bytes 1572872 | tf_op jit(solution)/shard_map/ppermute | solution.py:130
  21.9 17.9 %collective-permute-start.1 = (f16[2,8,128,128]{3,2,1,0:T(8,128)(2,1)S(1)}, f16[2,8,128,128]{3,2,1,0:T(8,128)(2,1)S(1)}, u32[]{:S(2)}, u32[]{:S(2)}) collective-permute-start(f16[2,8,128,128]{3,2,1,0:T(8,128)(2,1)S(1)} %get-tuple-element.17), channel_id=1, source_target_pairs={{0,128},{1,17},{2,130},{3,19},{4,132},{5,21},{6,134},{7,23},{8,136... | collective-permute-start | bytes 1572872 | tf_op jit(solution)/shard_map/ppermute | solution.py:130
  23.1 26.5 %collective-permute-start.3 = (f16[2,8,128,128]{3,2,1,0:T(8,128)(2,1)S(1)}, f16[2,8,128,128]{3,2,1,0:T(8,128)(2,1)S(1)}, u32[]{:S(2)}, u32[]{:S(2)}) collective-permute-start(f16[2,8,128,128]{3,2,1,0:T(8,128)(2,1)S(1)} %get-tuple-element.18), channel_id=1, source_target_pairs={{0,192},{1,49},{2,194},{3,51},{4,196},{5,53},{6,198},{7,55},{8,200... | collective-permute-start | bytes 1572872 | tf_op jit(solution)/shard_map/ppermute | solution.py:130
  27.0 27.8 %collective-permute-start.2 = (f16[2,8,128,128]{3,2,1,0:T(8,128)(2,1)S(1)}, f16[2,8,128,128]{3,2,1,0:T(8,128)(2,1)S(1)}, u32[]{:S(2)}, u32[]{:S(2)}) collective-permute-start(f16[2,8,128,128]{3,2,1,0:T(8,128)(2,1)S(1)} %get-tuple-element.19), channel_id=1, source_target_pairs={{0,64},{1,33},{2,66},{3,35},{4,68},{5,37},{6,70},{7,39},{8,72},{9,... | collective-permute-start | bytes 1572872 | tf_op jit(solution)/shard_map/ppermute | solution.py:130
  33.3 22.7 %collective-permute-start.8 = (f32[8,128,128]{2,1,0:T(8,128)S(1)}, f32[8,128,128]{2,1,0:T(8,128)S(1)}, u32[]{:S(2)}, u32[]{:S(2)}) collective-permute-start(f32[8,128,128]{2,1,0:T(8,128)S(1)} %get-tuple-element.20), channel_id=1, source_target_pairs={{0,16},{1,129},{2,18},{3,131},{4,20},{5,133},{6,22},{7,135},{8,24}... | collective-permute-start | bytes 1572872 | tf_op jit(solution)/shard_map/ppermute | solution.py:140
  35.3 20.6 %collective-permute-start.9 = (f32[8,128,128]{2,1,0:T(8,128)S(1)}, f32[8,128,128]{2,1,0:T(8,128)S(1)}, u32[]{:S(2)}, u32[]{:S(2)}) collective-permute-start(f32[8,128,128]{2,1,0:T(8,128)S(1)} %get-tuple-element.21), channel_id=1, source_target_pairs={{0,32},{1,65},{2,34},{3,67},{4,36},{5,69},{6,38},{7,71},{8,40},{9,... | collective-permute-start | bytes 1572872 | tf_op jit(solution)/shard_map/ppermute | solution.py:140
  55.3 34.1 %copy-start = (f32[16384]{0:T(1024)S(1)}, f32[16384]{0:T(1024)}, u32[]{:S(2)}) copy-start(f32[16384]{0:T(1024)} %param.5) | copy-start | bytes 196612
  55.4 34.1 %copy-start.1 = (f32[16384]{0:T(1024)S(1)}, f32[16384]{0:T(1024)}, u32[]{:S(2)}) copy-start(f32[16384]{0:T(1024)} %param.6) | copy-start | bytes 196612
  55.4 34.1 %copy-start.2 = (f32[16384]{0:T(1024)S(1)}, f32[16384]{0:T(1024)}, u32[]{:S(2)}) copy-start(f32[16384]{0:T(1024)} %param.7) | copy-start | bytes 196612
  55.4 9.3 %collective-permute-start.10 = (f32[8,128,128]{2,1,0:T(8,128)S(1)}, f32[8,128,128]{2,1,0:T(8,128)S(1)}, u32[]{:S(2)}, u32[]{:S(2)}) collective-permute-start(f32[8,128,128]{2,1,0:T(8,128)S(1)} %slice_bitcast_fusion), channel_id=1, source_target_pairs={{0,48},{1,193},{2,50},{3,195},{4,52},{5,197},{6,54},{7,199},{8,56}... | collective-permute-start | bytes 1572872 | tf_op jit(solution)/shard_map/ppermute | solution.py:140

commit v2 on v1

v2 whole, which is shorter than its diff:
```python
import functools

import jax
import jax.numpy as jnp
from jax import lax
from jax.experimental import pallas as pl
from jax.experimental.pallas import tpu as pltpu
from jax.sharding import Mesh, PartitionSpec as P

SHARD = 16384
LANES = 128
ROWS = SHARD // LANES
NX, NYL, NYH, NZ, NCORE = 4, 2, 2, 8, 2
NY = NYL * NYH
AXES = ("x", "ylo", "yhi", "z", "core")
GROUP = NZ * SHARD
LARGEST = 16.0
CHUNKS = ((2,), (1, 3), (0,))


def device_index(x, y, z, core):
    return (((x * NYL + y % NYL) * NYH + y // NYL) * NZ + z) * NCORE + core


def permutation(offset, stage):
    pairs = []
    for x in range(NX):
        for y in range(NY):
            for z in range(NZ):
                for core in range(NCORE):
                    if core == stage:
                        to = device_index((x + offset) % NX, y, z, core)
                    else:
                        to = device_index(x, (y + offset) % NY, z, core)
                    pairs.append((device_index(x, y, z, core), to))
    return pairs


SWAP = [(d, d ^ 1) for d in range(NX * NY * NZ * NCORE)]


def repack_kernel(chunk, grads, send, keep, raw, in_sem):
    x = lax.axis_index("x")
    y = lax.axis_index("yhi") * NYL + lax.axis_index("ylo")
    core = lax.axis_index("core")
    groups = [(half, j, first) for j in range(len(chunk)) for half in range(2) for first in range(4)]

    def start(i):
        half, j, first = groups[i]
        owner = core if half else 1 - core
        dx = jnp.where(owner == 0, first, chunk[j])
        dy = jnp.where(owner == 0, chunk[j], first)
        gx = lax.rem(x + dx, NX)
        gy = lax.rem(y + dy, NY)
        base = ((gx * NYL + lax.rem(gy, NYL)) * NYH + gy // NYL) * (NZ * NCORE) + owner
        for z in range(NZ):
            at = pl.multiple_of((base + z * NCORE) * SHARD, SHARD)
            pltpu.make_async_copy(
                grads.at[:, pl.ds(at, SHARD)],
                raw.at[:, pl.ds(i * GROUP + z * SHARD, SHARD)],
                in_sem.at[i],
            ).start()

    ahead = 8
    for i in range(min(ahead, len(groups))):
        start(i)
    for i, (half, j, first) in enumerate(groups):
        if i + ahead < len(groups):
            start(i + ahead)
        pltpu.make_async_copy(
            grads.at[:, pl.ds(0, GROUP)], raw.at[:, pl.ds(i * GROUP, GROUP)], in_sem.at[i]
        ).wait()
        out = keep if half else send
        for z in range(NZ):
            here = i * GROUP + z * SHARD
            wide = raw[:, pl.ds(here, SHARD)].astype(jnp.float32)
            out[first, j, z] = wide.reshape(ROWS, LANES).astype(jnp.bfloat16)


def repack(grads, chunk):
    n = len(chunk)
    shape = pltpu.VMEM((4, n, NZ, ROWS, LANES), jnp.bfloat16)
    return pl.pallas_call(
        functools.partial(repack_kernel, chunk),
        out_shape=(shape, shape),
        in_specs=[pl.BlockSpec(memory_space=pl.ANY)],
        out_specs=(pl.BlockSpec(memory_space=pltpu.VMEM),) * 2,
        scratch_shapes=[
            pltpu.VMEM((1, 8 * n * GROUP), jnp.bfloat16),
            pltpu.SemaphoreType.DMA((8 * n,)),
        ],
        compiler_params=pltpu.CompilerParams(vmem_limit_bytes=52 << 20),
        cost_estimate=pl.CostEstimate(
            flops=0, bytes_accessed=8 * n * GROUP * 6, transcendentals=0
        ),
    )(grads)


def encode_pair(value):
    return (value * 1024.0).astype(jnp.float16)


def decode_pair(value):
    return value.astype(jnp.float32) * (1.0 / 1024.0)


def scales(devices):
    limit = devices * LARGEST
    return limit / 256.0, 32768.0 / (limit * limit)


def encode(value, devices):
    knee, scale = scales(devices)
    return (value * jnp.maximum(jnp.abs(value), knee) * scale).astype(jnp.float16)


def decode(value, devices):
    knee, scale = scales(devices)
    wide = value.astype(jnp.float32)
    size = jnp.abs(wide)
    root = jnp.sqrt(size * (1.0 / scale))
    root = jnp.where(wide < 0, -root, root)
    return jnp.where(size < knee * knee * scale, wide * (1.0 / (knee * scale)), root)


def first_stage(send, keep, chunk):
    got = lax.ppermute(send, AXES, SWAP)

    def pair(k):
        return keep[k].astype(jnp.float32) + got[k].astype(jnp.float32)

    total = pair(0)
    for k in (2, 1, 3):
        total = total + decode_pair(
            lax.ppermute(encode_pair(pair(k)), AXES, permutation(k, 0))
        )
    return {q: total[j] for j, q in enumerate(chunk)}


def per_device(grads, params, moment_one, moment_two):
    parts = {}
    packed = []
    for chunk in CHUNKS:
        send, keep = repack(grads, chunk)
        grads, send = lax.optimization_barrier((grads, send))
        packed.append((send, keep))
    for chunk, (send, keep) in zip(CHUNKS, packed):
        parts.update(first_stage(send, keep, chunk))
    total = parts[0]
    for k in (2, 1, 3):
        total = total + decode(
            lax.ppermute(encode(parts[k], 8), AXES, permutation(k, 1)), 8
        )
    arrived = lax.all_to_all(
        encode(total, 32), "z", split_axis=0, concat_axis=0, tiled=True
    )
    summed = jnp.sum(decode(arrived, 32), axis=0).reshape(SHARD)
    new_one = 0.9 * moment_one + 0.1 * summed
    new_two = 0.999 * moment_two + 0.001 * summed * summed
    update = new_one / (1.0 - 0.9**10) / (jnp.sqrt(new_two / (1.0 - 0.999**10)) + 1e-08)
    return (params - 0.1 * update, new_one, new_two)


def solution(mesh):
    split = Mesh(mesh.devices.reshape(NX, NYL, NYH, NZ, NCORE), AXES)
    in_specs = (P(AXES, None), P(AXES), P(AXES), P(AXES))
    out_specs = (P(AXES), P(AXES), P(AXES))
    return jax.shard_map(
        per_device, mesh=split, in_specs=in_specs, out_specs=out_specs, check_vma=False
    )
```

time: 90.3 us -> 70.8 us (0.78)
  waiting for transfers between devices: 33.6 us -> 17.2 us
  Pallas kernels: 14.3 us -> 8.62 us
  starting transfers between devices: 13.6 us -> 18 us
  blocking collectives: 24.6 us -> 20.7 us
  other arithmetic: 3.04 us -> 4.6 us
    ppermute x9 -> x12, waiting for transfers between devices: 33.6 us -> 14.6 us  [the longest x9 14.5 us: first_stage(): lax.ppermute(encode_pair(pair(k)), AXES, permutation(k, 0))]
    pallas_call x2 -> x3, Pallas kernels: 14.3 us -> 8.62 us  [repack(): pl.pallas_call(functools.partial(repack_kernel, chunk), out_shape=(shape,...]
    ppermute x9 -> x12, starting transfers between devices: 13.1 us -> 17.2 us  [the longest x9 14 us: first_stage(): lax.ppermute(encode_pair(pair(k)), AXES, permutation(k, 0))]
    all_to_all x1, blocking collectives: 24.6 us -> 20.7 us  [per_device(): lax.all_to_all(encode(total, 32), 'z', split_axis=0, concat_axis=0, tiled...]
    ppermute x2 -> x3, waiting for transfers between devices: 0.01 us -> 2.59 us  [first_stage(): got = lax.ppermute(send, AXES, SWAP)]
    convert_element_type x2 -> x6, other arithmetic: 1.24 us -> 3.14 us  [the longest x3 1.67 us: encode(): (value * jnp.maximum(jnp.abs(value), knee) * scale).astype(jnp.float16)]
  transfers between devices with their start and end apart: 11 -> 15, of which waited for: 6 -> 8; matrix products, arithmetic and copies ran while one was open for 3% -> 4% of each run, Pallas kernels for 8% -> 3%
where the time goes in v2:
time: 70.8 us; the launch traced here: 69.9 us
  blocking collectives  20.7 us (29%)
  starting transfers between devices  18 us (25%)
  waiting for transfers between devices  17.2 us (24%)
  Pallas kernels  8.62 us (12%)
  other arithmetic  4.6 us (6%)
  between operations  0.78 us (1%)
    all_to_all x1, blocking collectives, per_device(): lax.all_to_all(encode(total, 32), 'z', split_axis=0, concat_axis=0, tiled...  20.7 us
    ppermute x9, waiting for transfers between devices, first_stage(): lax.ppermute(encode_pair(pair(k)), AXES, permutation(k, 0))  14.5 us
    ppermute x9, starting transfers between devices, first_stage(): lax.ppermute(encode_pair(pair(k)), AXES, permutation(k, 0))  14 us
    pallas_call x3, Pallas kernels, repack(): pl.pallas_call(functools.partial(repack_kernel, chunk), out_shape=(shape,...  8.62 us
    ppermute x3, starting transfers between devices, per_device(): lax.ppermute(encode(parts[k], 8), AXES, permutation(k, 1))  3.3 us
    ppermute x3, waiting for transfers between devices, first_stage(): got = lax.ppermute(send, AXES, SWAP)  2.59 us
    convert_element_type x3, other arithmetic, encode(): (value * jnp.maximum(jnp.abs(value), knee) * scale).astype(jnp.float16)  1.67 us
    convert_element_type x3, other arithmetic, encode_pair(): return (value * 1024.0).astype(jnp.float16)  1.47 us
  transfers between devices with their start and end apart: 15, of which 8 were waited for; matrix products, arithmetic and copies ran while one was open for 4% of the time, Pallas kernels for 3%

profile of v2, /device:TPU:16, one launch (start us, length us, event | category | flops | bytes accessed | tf_op | source)
XLA Modules:
  0.0 69.9 jit_solution(17426750144525362653)
XLA Ops:
  0.6 2.4 %shard_map.67 = (bf16[4,1,8,128,128]{4,3,2,1,0:T(8,128)(2,1)S(1)}, bf16[4,1,8,128,128]{4,3,2,1,0:T(8,128)(2,1)S(1)}) custom-call(bf16[1,4194304]{1,0:T(2,128)(2,1)} %grads.3), custom_call_target="tpu_custom_call" | custom-call | bytes 6291456 | tf_op jit(solution)/shard_map/pallas_call | solution.py:83
  3.0 3.8 %shard_map.68 = (bf16[4,2,8,128,128]{4,3,2,1,0:T(8,128)(2,1)S(1)}, bf16[4,2,8,128,128]{4,3,2,1,0:T(8,128)(2,1)S(1)}) custom-call(bf16[1,4194304]{1,0:T(2,128)(2,1)} %grads.3), custom_call_target="tpu_custom_call" | custom-call | bytes 12582912 | tf_op jit(solution)/shard_map/pallas_call | solution.py:83
  6.9 0.1 collective-permute-start.9
  7.0 0.5 collective-permute-start.4
  7.5 2.4 %shard_map.69 = (bf16[4,1,8,128,128]{4,3,2,1,0:T(8,128)(2,1)S(1)}, bf16[4,1,8,128,128]{4,3,2,1,0:T(8,128)(2,1)S(1)}) custom-call(bf16[1,4194304]{1,0:T(2,128)(2,1)} %grads.3), custom_call_target="tpu_custom_call" | custom-call | bytes 6291456 | tf_op jit(solution)/shard_map/pallas_call | solution.py:83
  9.9 0.2 collective-permute-start
  10.1 2.6 %collective-permute-done.4 = bf16[4,1,8,128,128]{4,3,2,1,0:T(8,128)(2,1)S(1)} collective-permute-done((bf16[4,1,8,128,128]{4,3,2,1,0:T(8,128)(2,1)S(1)}, bf16[4,1,8,128,128]{4,3,2,1,0:T(8,128)(2,1)S(1)}, u32[]{:S(2)}, u32[]{:S(2)}) %collective-permute-start.4) | collective-permute-done | bytes 1048608 | tf_op jit(solution)/shard_map/ppermute | solution.py:127
  12.6 0.3 fusion.32
  13.0 3.1 %collective-permute-start.5 = (f16[1,8,128,128]{3,2,1,0:T(8,128)(2,1)S(1)}, f16[1,8,128,128]{3,2,1,0:T(8,128)(2,1)S(1)}, u32[]{:S(2)}, u32[]{:S(2)}) collective-permute-start(f16[1,8,128,128]{3,2,1,0:T(8,128)(2,1)S(1)} %get-tuple-element.34), channel_id=1, source_target_pairs={{0,128},{1,17},{2,130},{3,19},{4,132},{5,21},{6,134},{7,23},{8,136... | collective-permute-start | bytes 786440 | tf_op jit(solution)/shard_map/ppermute | solution.py:135
  16.1 0.6 collective-permute-start.6
  16.7 2.6 %collective-permute-start.7 = (f16[1,8,128,128]{3,2,1,0:T(8,128)(2,1)S(1)}, f16[1,8,128,128]{3,2,1,0:T(8,128)(2,1)S(1)}, u32[]{:S(2)}, u32[]{:S(2)}) collective-permute-start(f16[1,8,128,128]{3,2,1,0:T(8,128)(2,1)S(1)} %get-tuple-element.35), channel_id=1, source_target_pairs={{0,192},{1,49},{2,194},{3,51},{4,196},{5,53},{6,198},{7,55},{8,200... | collective-permute-start | bytes 786440 | tf_op jit(solution)/shard_map/ppermute | solution.py:135
  19.3 0.0 collective-permute-done.9
  19.3 0.8 %fusion.19 = (f16[2,8,128,128]{3,2,1,0:T(8,128)(2,1)S(1)}, f16[2,8,128,128]{3,2,1,0:T(8,128)(2,1)S(1)}, f16[2,8,128,128]{3,2,1,0:T(8,128)(2,1)S(1)}) fusion(bf16[4,2,8,128,128]{4,3,2,1,0:T(8,128)(2,1)S(1)} %collective-permute-done.9, bf16[4,2,8,128,128]{4,3,2,1,0:T(8,128)(2,1)S(1)} %get-tuple-element.23), kind=kLoop, calls=%fused_computation.39 | loop fusion | flops 3932160 | bytes 4718592 | tf_op jit(solution)/shard_map/convert_element_type | solution.py:100
  20.2 0.1 collective-permute-start.10
  20.3 0.0 collective-permute-done
  20.3 0.8 %collective-permute-start.11 = (f16[2,8,128,128]{3,2,1,0:T(8,128)(2,1)S(1)}, f16[2,8,128,128]{3,2,1,0:T(8,128)(2,1)S(1)}, u32[]{:S(2)}, u32[]{:S(2)}) collective-permute-start(f16[2,8,128,128]{3,2,1,0:T(8,128)(2,1)S(1)} %get-tuple-element.30), channel_id=1, source_target_pairs={{0,64},{1,33},{2,66},{3,35},{4,68},{5,37},{6,70},{7,39},{8,72},{9,... | collective-permute-start | bytes 1572872 | tf_op jit(solution)/shard_map/ppermute | solution.py:135
  21.1 0.0 collective-permute-done.5
  21.1 2.6 %collective-permute-start.12 = (f16[2,8,128,128]{3,2,1,0:T(8,128)(2,1)S(1)}, f16[2,8,128,128]{3,2,1,0:T(8,128)(2,1)S(1)}, u32[]{:S(2)}, u32[]{:S(2)}) collective-permute-start(f16[2,8,128,128]{3,2,1,0:T(8,128)(2,1)S(1)} %get-tuple-element.29), channel_id=1, source_target_pairs={{0,192},{1,49},{2,194},{3,51},{4,196},{5,53},{6,198},{7,55},{8,200... | collective-permute-start | bytes 1572872 | tf_op jit(solution)/shard_map/ppermute | solution.py:135
  23.7 0.3 fusion.29
  24.0 0.0 collective-permute-done.6
  24.0 2.2 %collective-permute-start.1 = (f16[1,8,128,128]{3,2,1,0:T(8,128)(2,1)S(1)}, f16[1,8,128,128]{3,2,1,0:T(8,128)(2,1)S(1)}, u32[]{:S(2)}, u32[]{:S(2)}) collective-permute-start(f16[1,8,128,128]{3,2,1,0:T(8,128)(2,1)S(1)} %get-tuple-element.31), channel_id=1, source_target_pairs={{0,128},{1,17},{2,130},{3,19},{4,132},{5,21},{6,134},{7,23},{8,136... | collective-permute-start | bytes 786440 | tf_op jit(solution)/shard_map/ppermute | solution.py:135
  26.2 2.6 %collective-permute-done.7 = f16[1,8,128,128]{3,2,1,0:T(8,128)(2,1)S(1)} collective-permute-done((f16[1,8,128,128]{3,2,1,0:T(8,128)(2,1)S(1)}, f16[1,8,128,128]{3,2,1,0:T(8,128)(2,1)S(1)}, u32[]{:S(2)}, u32[]{:S(2)}) %collective-permute-start.7) | collective-permute-done | bytes 262176 | tf_op jit(solution)/shard_map/ppermute | solution.py:135
  28.9 0.0 collective-permute-start.2
  28.9 0.3 fusion.24
  29.2 1.9 %collective-permute-done.10 = f16[2,8,128,128]{3,2,1,0:T(8,128)(2,1)S(1)} collective-permute-done((f16[2,8,128,128]{3,2,1,0:T(8,128)(2,1)S(1)}, f16[2,8,128,128]{3,2,1,0:T(8,128)(2,1)S(1)}, u32[]{:S(2)}, u32[]{:S(2)}) %collective-permute-start.10) | collective-permute-done | bytes 524320 | tf_op jit(solution)/shard_map/ppermute | solution.py:135
  31.1 1.9 %collective-permute-start.3 = (f16[1,8,128,128]{3,2,1,0:T(8,128)(2,1)S(1)}, f16[1,8,128,128]{3,2,1,0:T(8,128)(2,1)S(1)}, u32[]{:S(2)}, u32[]{:S(2)}) collective-permute-start(f16[1,8,128,128]{3,2,1,0:T(8,128)(2,1)S(1)} %get-tuple-element.32), channel_id=1, source_target_pairs={{0,192},{1,49},{2,194},{3,51},{4,196},{5,53},{6,198},{7,55},{8,200... | collective-permute-start | bytes 786440 | tf_op jit(solution)/shard_map/ppermute | solution.py:135
  32.9 3.4 %collective-permute-done.11 = f16[2,8,128,128]{3,2,1,0:T(8,128)(2,1)S(1)} collective-permute-done((f16[2,8,128,128]{3,2,1,0:T(8,128)(2,1)S(1)}, f16[2,8,128,128]{3,2,1,0:T(8,128)(2,1)S(1)}, u32[]{:S(2)}, u32[]{:S(2)}) %collective-permute-start.11) | collective-permute-done | bytes 524320 | tf_op jit(solution)/shard_map/ppermute | solution.py:135
  36.4 0.7 %collective-permute-start.8 = (f16[8,128,128]{2,1,0:T(8,128)(2,1)S(1)}, f16[8,128,128]{2,1,0:T(8,128)(2,1)S(1)}, u32[]{:S(2)}, u32[]{:S(2)}) collective-permute-start(f16[8,128,128]{2,1,0:T(8,128)(2,1)S(1)} %fusion.24), channel_id=1, source_target_pairs={{0,16},{1,129},{2,18},{3,131},{4,20},{5,133},{6,22},{7,135},{8,24}... | collective-permute-start | bytes 786440 | tf_op jit(solution)/shard_map/ppermute | solution.py:152
  37.1 0.3 collective-permute-done.12
  37.4 0.5 fusion.1
  37.9 0.0 copy-start
  37.9 0.0 copy-start.1
  37.9 0.0 copy-start.2
  37.9 0.2 multiply_convert_fusion.5
  38.2 2.3 %collective-permute-start.13 = (f16[8,128,128]{2,1,0:T(8,128)(2,1)S(1)}, f16[8,128,128]{2,1,0:T(8,128)(2,1)S(1)}, u32[]{:S(2)}, u32[]{:S(2)}) collective-permute-start(f16[8,128,128]{2,1,0:T(8,128)(2,1)S(1)} %get-tuple-element.37), channel_id=1, source_target_pairs={{0,32},{1,65},{2,34},{3,67},{4,36},{5,69},{6,38},{7,71},{8,40},{9,... | collective-permute-start | bytes 786440 | tf_op jit(solution)/shard_map/ppermute | solution.py:152
  40.5 0.1 collective-permute-done.1
  40.5 0.2 collective-permute-start.14
  40.8 6.2 %collective-permute-done.2 = f16[1,8,128,128]{3,2,1,0:T(8,128)(2,1)S(1)} collective-permute-done((f16[1,8,128,128]{3,2,1,0:T(8,128)(2,1)S(1)}, f16[1,8,128,128]{3,2,1,0:T(8,128)(2,1)S(1)}, u32[]{:S(2)}, u32[]{:S(2)}) %collective-permute-start.2) | collective-permute-done | bytes 262176 | tf_op jit(solution)/shard_map/ppermute | solution.py:135
  47.0 0.0 collective-permute-done.3
  47.0 0.0 collective-permute-done.8
  47.0 0.1 collective-permute-done.13
  47.1 0.0 collective-permute-done.14
  47.1 1.1 %multiply_convert_fusion.3 = f16[8,128,128]{2,1,0:T(8,128)(2,1)S(1)} fusion(f16[8,128,128]{2,1,0:T(8,128)(2,1)S(1)} %collective-permute-done.14, f16[8,128,128]{2,1,0:T(8,128)(2,1)S(1)} %collective-permute-done.13, f16[8,128,128]{2,1,0:T(8,128)(2,1)S(1)} %collective-permute-done.8, f16[1,8,128,128]{3,2,1,0:T(8,128)(2,1)S(1)} %collective-permute-done.3, ...), kind=kLoop, calls=%fused_computation.55 | loop fusion | flops 5767168 | bytes 2359296 | tf_op jit(solution)/shard_map/convert_element_type | solution.py:114
  48.2 20.7 %all_to_all.5 = f16[8,128,128]{2,1,0:T(8,128)(2,1)S(1)} all-to-all(f16[8,128,128]{2,1,0:T(8,128)(2,1)S(1)} %multiply_convert_fusion.3), channel_id=1, replica_groups=mesh['x'=4,'ylo'=2,'yhi'=2,'z'=8,'core'=2] {'z'}, dimensions={0} | all-to-all | bytes 524288 | tf_op jit(solution)/shard_map/all_to_all | solution.py:154
  68.9 0.3 fusion.18
  69.2 0.0 copy-done
  69.2 0.0 copy-done.1
  69.2 0.0 copy-done.2
  69.2 0.7 multiply_subtract_fusion
Async XLA Ops:
  6.9 12.4 %collective-permute-start.9 = (bf16[4,2,8,128,128]{4,3,2,1,0:T(8,128)(2,1)S(1)}, bf16[4,2,8,128,128]{4,3,2,1,0:T(8,128)(2,1)S(1)}, u32[]{:S(2)}, u32[]{:S(2)}) collective-permute-start(bf16[4,2,8,128,128]{4,3,2,1,0:T(8,128)(2,1)S(1)} %get-tuple-element.24), channel_id=1, source_target_pairs={{0,1},{1,0},{2,3},{3,2},{4,5},{5,4},{6,7},{7,6},{8,9},{9,8},{10,11... | collective-permute-start | bytes 6291464 | tf_op jit(solution)/shard_map/ppermute | solution.py:127
  7.0 5.6 %collective-permute-start.4 = (bf16[4,1,8,128,128]{4,3,2,1,0:T(8,128)(2,1)S(1)}, bf16[4,1,8,128,128]{4,3,2,1,0:T(8,128)(2,1)S(1)}, u32[]{:S(2)}, u32[]{:S(2)}) collective-permute-start(bf16[4,1,8,128,128]{4,3,2,1,0:T(8,128)(2,1)S(1)} %get-tuple-element.22), channel_id=1, source_target_pairs={{0,1},{1,0},{2,3},{3,2},{4,5},{5,4},{6,7},{7,6},{8,9},{9,8},{10,11... | collective-permute-start | bytes 3145736 | tf_op jit(solution)/shard_map/ppermute | solution.py:127
  9.9 10.4 %collective-permute-start = (bf16[4,1,8,128,128]{4,3,2,1,0:T(8,128)(2,1)S(1)}, bf16[4,1,8,128,128]{4,3,2,1,0:T(8,128)(2,1)S(1)}, u32[]{:S(2)}, u32[]{:S(2)}) collective-permute-start(bf16[4,1,8,128,128]{4,3,2,1,0:T(8,128)(2,1)S(1)} %get-tuple-element.20), channel_id=1, source_target_pairs={{0,1},{1,0},{2,3},{3,2},{4,5},{5,4},{6,7},{7,6},{8,9},{9,8},{10,11... | collective-permute-start | bytes 3145736 | tf_op jit(solution)/shard_map/ppermute | solution.py:127
  13.0 8.1 %collective-permute-start.5 = (f16[1,8,128,128]{3,2,1,0:T(8,128)(2,1)S(1)}, f16[1,8,128,128]{3,2,1,0:T(8,128)(2,1)S(1)}, u32[]{:S(2)}, u32[]{:S(2)}) collective-permute-start(f16[1,8,128,128]{3,2,1,0:T(8,128)(2,1)S(1)} %get-tuple-element.34), channel_id=1, source_target_pairs={{0,128},{1,17},{2,130},{3,19},{4,132},{5,21},{6,134},{7,23},{8,136... | collective-permute-start | bytes 786440 | tf_op jit(solution)/shard_map/ppermute | solution.py:135
  16.1 7.9 %collective-permute-start.6 = (f16[1,8,128,128]{3,2,1,0:T(8,128)(2,1)S(1)}, f16[1,8,128,128]{3,2,1,0:T(8,128)(2,1)S(1)}, u32[]{:S(2)}, u32[]{:S(2)}) collective-permute-start(f16[1,8,128,128]{3,2,1,0:T(8,128)(2,1)S(1)} %get-tuple-element.36), channel_id=1, source_target_pairs={{0,64},{1,33},{2,66},{3,35},{4,68},{5,37},{6,70},{7,39},{8,72},{9,... | collective-permute-start | bytes 786440 | tf_op jit(solution)/shard_map/ppermute | solution.py:135
  16.7 12.2 %collective-permute-start.7 = (f16[1,8,128,128]{3,2,1,0:T(8,128)(2,1)S(1)}, f16[1,8,128,128]{3,2,1,0:T(8,128)(2,1)S(1)}, u32[]{:S(2)}, u32[]{:S(2)}) collective-permute-start(f16[1,8,128,128]{3,2,1,0:T(8,128)(2,1)S(1)} %get-tuple-element.35), channel_id=1, source_target_pairs={{0,192},{1,49},{2,194},{3,51},{4,196},{5,53},{6,198},{7,55},{8,200... | collective-permute-start | bytes 786440 | tf_op jit(solution)/shard_map/ppermute | solution.py:135
  20.2 10.9 %collective-permute-start.10 = (f16[2,8,128,128]{3,2,1,0:T(8,128)(2,1)S(1)}, f16[2,8,128,128]{3,2,1,0:T(8,128)(2,1)S(1)}, u32[]{:S(2)}, u32[]{:S(2)}) collective-permute-start(f16[2,8,128,128]{3,2,1,0:T(8,128)(2,1)S(1)} %get-tuple-element.28), channel_id=1, source_target_pairs={{0,128},{1,17},{2,130},{3,19},{4,132},{5,21},{6,134},{7,23},{8,136... | collective-permute-start | bytes 1572872 | tf_op jit(solution)/shard_map/ppermute | solution.py:135
  20.3 16.1 %collective-permute-start.11 = (f16[2,8,128,128]{3,2,1,0:T(8,128)(2,1)S(1)}, f16[2,8,128,128]{3,2,1,0:T(8,128)(2,1)S(1)}, u32[]{:S(2)}, u32[]{:S(2)}) collective-permute-start(f16[2,8,128,128]{3,2,1,0:T(8,128)(2,1)S(1)} %get-tuple-element.30), channel_id=1, source_target_pairs={{0,64},{1,33},{2,66},{3,35},{4,68},{5,37},{6,70},{7,39},{8,72},{9,... | collective-permute-start | bytes 1572872 | tf_op jit(solution)/shard_map/ppermute | solution.py:135
  21.1 16.3 %collective-permute-start.12 = (f16[2,8,128,128]{3,2,1,0:T(8,128)(2,1)S(1)}, f16[2,8,128,128]{3,2,1,0:T(8,128)(2,1)S(1)}, u32[]{:S(2)}, u32[]{:S(2)}) collective-permute-start(f16[2,8,128,128]{3,2,1,0:T(8,128)(2,1)S(1)} %get-tuple-element.29), channel_id=1, source_target_pairs={{0,192},{1,49},{2,194},{3,51},{4,196},{5,53},{6,198},{7,55},{8,200... | collective-permute-start | bytes 1572872 | tf_op jit(solution)/shard_map/ppermute | solution.py:135
  24.0 16.5 %collective-permute-start.1 = (f16[1,8,128,128]{3,2,1,0:T(8,128)(2,1)S(1)}, f16[1,8,128,128]{3,2,1,0:T(8,128)(2,1)S(1)}, u32[]{:S(2)}, u32[]{:S(2)}) collective-permute-start(f16[1,8,128,128]{3,2,1,0:T(8,128)(2,1)S(1)} %get-tuple-element.31), channel_id=1, source_target_pairs={{0,128},{1,17},{2,130},{3,19},{4,132},{5,21},{6,134},{7,23},{8,136... | collective-permute-start | bytes 786440 | tf_op jit(solution)/shard_map/ppermute | solution.py:135
  28.9 18.1 %collective-permute-start.2 = (f16[1,8,128,128]{3,2,1,0:T(8,128)(2,1)S(1)}, f16[1,8,128,128]{3,2,1,0:T(8,128)(2,1)S(1)}, u32[]{:S(2)}, u32[]{:S(2)}) collective-permute-start(f16[1,8,128,128]{3,2,1,0:T(8,128)(2,1)S(1)} %get-tuple-element.33), channel_id=1, source_target_pairs={{0,64},{1,33},{2,66},{3,35},{4,68},{5,37},{6,70},{7,39},{8,72},{9,... | collective-permute-start | bytes 786440 | tf_op jit(solution)/shard_map/ppermute | solution.py:135
  31.1 15.9 %collective-permute-start.3 = (f16[1,8,128,128]{3,2,1,0:T(8,128)(2,1)S(1)}, f16[1,8,128,128]{3,2,1,0:T(8,128)(2,1)S(1)}, u32[]{:S(2)}, u32[]{:S(2)}) collective-permute-start(f16[1,8,128,128]{3,2,1,0:T(8,128)(2,1)S(1)} %get-tuple-element.32), channel_id=1, source_target_pairs={{0,192},{1,49},{2,194},{3,51},{4,196},{5,53},{6,198},{7,55},{8,200... | collective-permute-start | bytes 786440 | tf_op jit(solution)/shard_map/ppermute | solution.py:135
  36.4 10.6 %collective-permute-start.8 = (f16[8,128,128]{2,1,0:T(8,128)(2,1)S(1)}, f16[8,128,128]{2,1,0:T(8,128)(2,1)S(1)}, u32[]{:S(2)}, u32[]{:S(2)}) collective-permute-start(f16[8,128,128]{2,1,0:T(8,128)(2,1)S(1)} %fusion.24), channel_id=1, source_target_pairs={{0,16},{1,129},{2,18},{3,131},{4,20},{5,133},{6,22},{7,135},{8,24}... | collective-permute-start | bytes 786440 | tf_op jit(solution)/shard_map/ppermute | solution.py:152
  37.9 31.3 %copy-start = (f32[16384]{0:T(1024)S(1)}, f32[16384]{0:T(1024)}, u32[]{:S(2)}) copy-start(f32[16384]{0:T(1024)} %param.5) | copy-start | bytes 196612
  37.9 31.3 %copy-start.1 = (f32[16384]{0:T(1024)S(1)}, f32[16384]{0:T(1024)}, u32[]{:S(2)}) copy-start(f32[16384]{0:T(1024)} %param.6) | copy-start | bytes 196612
  37.9 31.3 %copy-start.2 = (f32[16384]{0:T(1024)S(1)}, f32[16384]{0:T(1024)}, u32[]{:S(2)}) copy-start(f32[16384]{0:T(1024)} %param.7) | copy-start | bytes 196612
  38.2 8.9 %collective-permute-start.13 = (f16[8,128,128]{2,1,0:T(8,128)(2,1)S(1)}, f16[8,128,128]{2,1,0:T(8,128)(2,1)S(1)}, u32[]{:S(2)}, u32[]{:S(2)}) collective-permute-start(f16[8,128,128]{2,1,0:T(8,128)(2,1)S(1)} %get-tuple-element.37), channel_id=1, source_target_pairs={{0,32},{1,65},{2,34},{3,67},{4,36},{5,69},{6,38},{7,71},{8,40},{9,... | collective-permute-start | bytes 786440 | tf_op jit(solution)/shard_map/ppermute | solution.py:152
  40.5 6.5 %collective-permute-start.14 = (f16[8,128,128]{2,1,0:T(8,128)(2,1)S(1)}, f16[8,128,128]{2,1,0:T(8,128)(2,1)S(1)}, u32[]{:S(2)}, u32[]{:S(2)}) collective-permute-start(f16[8,128,128]{2,1,0:T(8,128)(2,1)S(1)} %get-tuple-element.38), channel_id=1, source_target_pairs={{0,48},{1,193},{2,50},{3,195},{4,52},{5,197},{6,54},{7,199},{8,56}... | collective-permute-start | bytes 786440 | tf_op jit(solution)/shard_map/ppermute | solution.py:152

commit v3 on v2

--- a/solution.py
+++ b/solution.py
@@ -15,7 +15,7 @@
 AXES = ("x", "ylo", "yhi", "z", "core")
 GROUP = NZ * SHARD
 LARGEST = 16.0
-CHUNKS = ((2,), (1, 3), (0,))
+CHUNKS = ((1, 3), (2,), (0,))
 
 
 def device_index(x, y, z, core):

time: 70.8 us -> 70.1 us (level)
  waiting for transfers between devices: 17.2 us -> 23.4 us
  starting transfers between devices: 18 us -> 13.3 us
  blocking collectives: 20.7 us -> 18.7 us
    ppermute x9, waiting for transfers between devices: 14.5 us -> 20.2 us  [first_stage(): lax.ppermute(encode_pair(pair(k)), AXES, permutation(k, 0))]
    ppermute x3, starting transfers between devices: 3.3 us -> 0.34 us  [per_device(): lax.ppermute(encode(parts[k], 8), AXES, permutation(k, 1))]
    ppermute x3, waiting for transfers between devices: 0.11 us -> 3.01 us  [per_device(): lax.ppermute(encode(parts[k], 8), AXES, permutation(k, 1))]
    ppermute x3, waiting for transfers between devices: 2.59 us -> 0.17 us  [first_stage(): got = lax.ppermute(send, AXES, SWAP)]
    all_to_all x1, blocking collectives: 20.7 us -> 18.7 us  [per_device(): lax.all_to_all(encode(total, 32), 'z', split_axis=0, concat_axis=0, tiled...]
    ppermute x9, starting transfers between devices: 14 us -> 12.2 us  [first_stage(): lax.ppermute(encode_pair(pair(k)), AXES, permutation(k, 0))]
  transfers between devices with their start and end apart: 15 -> 15, of which waited for: 8 -> 10; matrix products, arithmetic and copies ran while one was open for 4% -> 4% of each run, Pallas kernels for 3% -> 7%
where the time goes in v3:
time: 70.1 us; the launch traced here: 69.4 us
  waiting for transfers between devices  23.4 us (33%)
  blocking collectives  18.7 us (27%)
  starting transfers between devices  13.3 us (19%)
  Pallas kernels  8.62 us (12%)
  other arithmetic  4.6 us (7%)
  between operations  0.76 us (1%)
    ppermute x9, waiting for transfers between devices, first_stage(): lax.ppermute(encode_pair(pair(k)), AXES, permutation(k, 0))  20.2 us
    all_to_all x1, blocking collectives, per_device(): lax.all_to_all(encode(total, 32), 'z', split_axis=0, concat_axis=0, tiled...  18.7 us
    ppermute x9, starting transfers between devices, first_stage(): lax.ppermute(encode_pair(pair(k)), AXES, permutation(k, 0))  12.2 us
    pallas_call x3, Pallas kernels, repack(): pl.pallas_call(functools.partial(repack_kernel, chunk), out_shape=(shape,...  8.62 us
    ppermute x3, waiting for transfers between devices, per_device(): lax.ppermute(encode(parts[k], 8), AXES, permutation(k, 1))  3.01 us
    convert_element_type x3, other arithmetic, encode(): (value * jnp.maximum(jnp.abs(value), knee) * scale).astype(jnp.float16)  1.67 us
    convert_element_type x3, other arithmetic, encode_pair(): return (value * 1024.0).astype(jnp.float16)  1.47 us
  transfers between devices with their start and end apart: 15, of which 10 were waited for; matrix products, arithmetic and copies ran while one was open for 4% of the time, Pallas kernels for 7%

profile of v3, /device:TPU:16, one launch (start us, length us, event | category | flops | bytes accessed | tf_op | source)
XLA Modules:
  0.0 69.4 jit_solution(2241045845822587509)
XLA Ops:
  0.6 3.8 %shard_map.67 = (bf16[4,2,8,128,128]{4,3,2,1,0:T(8,128)(2,1)S(1)}, bf16[4,2,8,128,128]{4,3,2,1,0:T(8,128)(2,1)S(1)}) custom-call(bf16[1,4194304]{1,0:T(2,128)(2,1)} %grads.3), custom_call_target="tpu_custom_call" | custom-call | bytes 12582912 | tf_op jit(solution)/shard_map/pallas_call | solution.py:83
  4.5 0.1 collective-permute-start.9
  4.6 2.4 %shard_map.68 = (bf16[4,1,8,128,128]{4,3,2,1,0:T(8,128)(2,1)S(1)}, bf16[4,1,8,128,128]{4,3,2,1,0:T(8,128)(2,1)S(1)}) custom-call(bf16[1,4194304]{1,0:T(2,128)(2,1)} %grads.3), custom_call_target="tpu_custom_call" | custom-call | bytes 6291456 | tf_op jit(solution)/shard_map/pallas_call | solution.py:83
  7.0 0.5 collective-permute-start.4
  7.5 2.4 %shard_map.69 = (bf16[4,1,8,128,128]{4,3,2,1,0:T(8,128)(2,1)S(1)}, bf16[4,1,8,128,128]{4,3,2,1,0:T(8,128)(2,1)S(1)}) custom-call(bf16[1,4194304]{1,0:T(2,128)(2,1)} %grads.3), custom_call_target="tpu_custom_call" | custom-call | bytes 6291456 | tf_op jit(solution)/shard_map/pallas_call | solution.py:83
  9.9 0.1 collective-permute-start
  10.1 0.2 collective-permute-done.4
  10.2 0.3 fusion.32
  10.6 2.8 %collective-permute-start.7 = (f16[1,8,128,128]{3,2,1,0:T(8,128)(2,1)S(1)}, f16[1,8,128,128]{3,2,1,0:T(8,128)(2,1)S(1)}, u32[]{:S(2)}, u32[]{:S(2)}) collective-permute-start(f16[1,8,128,128]{3,2,1,0:T(8,128)(2,1)S(1)} %get-tuple-element.35), channel_id=1, source_target_pairs={{0,192},{1,49},{2,194},{3,51},{4,196},{5,53},{6,198},{7,55},{8,200... | collective-permute-start | bytes 786440 | tf_op jit(solution)/shard_map/ppermute | solution.py:135
  13.4 0.0 collective-permute-start.6
  13.4 2.3 %collective-permute-start.5 = (f16[1,8,128,128]{3,2,1,0:T(8,128)(2,1)S(1)}, f16[1,8,128,128]{3,2,1,0:T(8,128)(2,1)S(1)}, u32[]{:S(2)}, u32[]{:S(2)}) collective-permute-start(f16[1,8,128,128]{3,2,1,0:T(8,128)(2,1)S(1)} %get-tuple-element.34), channel_id=1, source_target_pairs={{0,128},{1,17},{2,130},{3,19},{4,132},{5,21},{6,134},{7,23},{8,136... | collective-permute-start | bytes 786440 | tf_op jit(solution)/shard_map/ppermute | solution.py:135
  15.7 0.0 collective-permute-done.9
  15.7 0.8 %fusion.19 = (f16[2,8,128,128]{3,2,1,0:T(8,128)(2,1)S(1)}, f16[2,8,128,128]{3,2,1,0:T(8,128)(2,1)S(1)}, f16[2,8,128,128]{3,2,1,0:T(8,128)(2,1)S(1)}) fusion(bf16[4,2,8,128,128]{4,3,2,1,0:T(8,128)(2,1)S(1)} %collective-permute-done.9, bf16[4,2,8,128,128]{4,3,2,1,0:T(8,128)(2,1)S(1)} %get-tuple-element.23), kind=kLoop, calls=%fused_computation.39 | loop fusion | flops 3932160 | bytes 4718592 | tf_op jit(solution)/shard_map/convert_element_type | solution.py:100
  16.5 1.2 %collective-permute-start.12 = (f16[2,8,128,128]{3,2,1,0:T(8,128)(2,1)S(1)}, f16[2,8,128,128]{3,2,1,0:T(8,128)(2,1)S(1)}, u32[]{:S(2)}, u32[]{:S(2)}) collective-permute-start(f16[2,8,128,128]{3,2,1,0:T(8,128)(2,1)S(1)} %get-tuple-element.29), channel_id=1, source_target_pairs={{0,192},{1,49},{2,194},{3,51},{4,196},{5,53},{6,198},{7,55},{8,200... | collective-permute-start | bytes 1572872 | tf_op jit(solution)/shard_map/ppermute | solution.py:135
  17.8 0.0 collective-permute-done
  17.8 0.9 %collective-permute-start.11 = (f16[2,8,128,128]{3,2,1,0:T(8,128)(2,1)S(1)}, f16[2,8,128,128]{3,2,1,0:T(8,128)(2,1)S(1)}, u32[]{:S(2)}, u32[]{:S(2)}) collective-permute-start(f16[2,8,128,128]{3,2,1,0:T(8,128)(2,1)S(1)} %get-tuple-element.30), channel_id=1, source_target_pairs={{0,64},{1,33},{2,66},{3,35},{4,68},{5,37},{6,70},{7,39},{8,72},{9,... | collective-permute-start | bytes 1572872 | tf_op jit(solution)/shard_map/ppermute | solution.py:135
  18.6 0.0 collective-permute-done.7
  18.6 1.9 %collective-permute-start.10 = (f16[2,8,128,128]{3,2,1,0:T(8,128)(2,1)S(1)}, f16[2,8,128,128]{3,2,1,0:T(8,128)(2,1)S(1)}, u32[]{:S(2)}, u32[]{:S(2)}) collective-permute-start(f16[2,8,128,128]{3,2,1,0:T(8,128)(2,1)S(1)} %get-tuple-element.28), channel_id=1, source_target_pairs={{0,128},{1,17},{2,130},{3,19},{4,132},{5,21},{6,134},{7,23},{8,136... | collective-permute-start | bytes 1572872 | tf_op jit(solution)/shard_map/ppermute | solution.py:135
  20.6 0.3 fusion.29
  20.9 2.9 %collective-permute-done.6 = f16[1,8,128,128]{3,2,1,0:T(8,128)(2,1)S(1)} collective-permute-done((f16[1,8,128,128]{3,2,1,0:T(8,128)(2,1)S(1)}, f16[1,8,128,128]{3,2,1,0:T(8,128)(2,1)S(1)}, u32[]{:S(2)}, u32[]{:S(2)}) %collective-permute-start.6) | collective-permute-done | bytes 262176 | tf_op jit(solution)/shard_map/ppermute | solution.py:135
  23.8 0.0 collective-permute-start.3
  23.8 0.0 collective-permute-done.5
  23.8 2.0 %collective-permute-start.2 = (f16[1,8,128,128]{3,2,1,0:T(8,128)(2,1)S(1)}, f16[1,8,128,128]{3,2,1,0:T(8,128)(2,1)S(1)}, u32[]{:S(2)}, u32[]{:S(2)}) collective-permute-start(f16[1,8,128,128]{3,2,1,0:T(8,128)(2,1)S(1)} %get-tuple-element.33), channel_id=1, source_target_pairs={{0,64},{1,33},{2,66},{3,35},{4,68},{5,37},{6,70},{7,39},{8,72},{9,... | collective-permute-start | bytes 786440 | tf_op jit(solution)/shard_map/ppermute | solution.py:135
  25.8 0.3 fusion.24
  26.1 1.4 %collective-permute-done.12 = f16[2,8,128,128]{3,2,1,0:T(8,128)(2,1)S(1)} collective-permute-done((f16[2,8,128,128]{3,2,1,0:T(8,128)(2,1)S(1)}, f16[2,8,128,128]{3,2,1,0:T(8,128)(2,1)S(1)}, u32[]{:S(2)}, u32[]{:S(2)}) %collective-permute-start.12) | collective-permute-done | bytes 524320 | tf_op jit(solution)/shard_map/ppermute | solution.py:135
  27.5 1.0 %collective-permute-start.1 = (f16[1,8,128,128]{3,2,1,0:T(8,128)(2,1)S(1)}, f16[1,8,128,128]{3,2,1,0:T(8,128)(2,1)S(1)}, u32[]{:S(2)}, u32[]{:S(2)}) collective-permute-start(f16[1,8,128,128]{3,2,1,0:T(8,128)(2,1)S(1)} %get-tuple-element.31), channel_id=1, source_target_pairs={{0,128},{1,17},{2,130},{3,19},{4,132},{5,21},{6,134},{7,23},{8,136... | collective-permute-start | bytes 786440 | tf_op jit(solution)/shard_map/ppermute | solution.py:135
  28.5 9.4 %collective-permute-done.11 = f16[2,8,128,128]{3,2,1,0:T(8,128)(2,1)S(1)} collective-permute-done((f16[2,8,128,128]{3,2,1,0:T(8,128)(2,1)S(1)}, f16[2,8,128,128]{3,2,1,0:T(8,128)(2,1)S(1)}, u32[]{:S(2)}, u32[]{:S(2)}) %collective-permute-start.11) | collective-permute-done | bytes 524320 | tf_op jit(solution)/shard_map/ppermute | solution.py:135
  37.8 0.0 collective-permute-start.8
  37.8 0.0 collective-permute-done.10
  37.8 0.5 fusion.1
  38.3 0.0 copy-start
  38.3 0.0 copy-start.1
  38.3 0.0 copy-start.2
  38.4 0.2 multiply_convert_fusion.5
  38.6 0.3 collective-permute-start.14
  38.9 2.1 %collective-permute-done.3 = f16[1,8,128,128]{3,2,1,0:T(8,128)(2,1)S(1)} collective-permute-done((f16[1,8,128,128]{3,2,1,0:T(8,128)(2,1)S(1)}, f16[1,8,128,128]{3,2,1,0:T(8,128)(2,1)S(1)}, u32[]{:S(2)}, u32[]{:S(2)}) %collective-permute-start.3) | collective-permute-done | bytes 262176 | tf_op jit(solution)/shard_map/ppermute | solution.py:135
  41.0 0.0 collective-permute-start.13
  41.1 2.3 %collective-permute-done.2 = f16[1,8,128,128]{3,2,1,0:T(8,128)(2,1)S(1)} collective-permute-done((f16[1,8,128,128]{3,2,1,0:T(8,128)(2,1)S(1)}, f16[1,8,128,128]{3,2,1,0:T(8,128)(2,1)S(1)}, u32[]{:S(2)}, u32[]{:S(2)}) %collective-permute-start.2) | collective-permute-done | bytes 262176 | tf_op jit(solution)/shard_map/ppermute | solution.py:135
  43.3 2.2 %collective-permute-done.1 = f16[1,8,128,128]{3,2,1,0:T(8,128)(2,1)S(1)} collective-permute-done((f16[1,8,128,128]{3,2,1,0:T(8,128)(2,1)S(1)}, f16[1,8,128,128]{3,2,1,0:T(8,128)(2,1)S(1)}, u32[]{:S(2)}, u32[]{:S(2)}) %collective-permute-start.1) | collective-permute-done | bytes 262176 | tf_op jit(solution)/shard_map/ppermute | solution.py:135
  45.5 0.3 collective-permute-done.8
  45.8 1.5 %collective-permute-done.14 = f16[8,128,128]{2,1,0:T(8,128)(2,1)S(1)} collective-permute-done((f16[8,128,128]{2,1,0:T(8,128)(2,1)S(1)}, f16[8,128,128]{2,1,0:T(8,128)(2,1)S(1)}, u32[]{:S(2)}, u32[]{:S(2)}) %collective-permute-start.14) | collective-permute-done | bytes 262176 | tf_op jit(solution)/shard_map/ppermute | solution.py:152
  47.3 1.2 %collective-permute-done.13 = f16[8,128,128]{2,1,0:T(8,128)(2,1)S(1)} collective-permute-done((f16[8,128,128]{2,1,0:T(8,128)(2,1)S(1)}, f16[8,128,128]{2,1,0:T(8,128)(2,1)S(1)}, u32[]{:S(2)}, u32[]{:S(2)}) %collective-permute-start.13) | collective-permute-done | bytes 262176 | tf_op jit(solution)/shard_map/ppermute | solution.py:152
  48.5 1.1 %multiply_convert_fusion.3 = f16[8,128,128]{2,1,0:T(8,128)(2,1)S(1)} fusion(f16[8,128,128]{2,1,0:T(8,128)(2,1)S(1)} %collective-permute-done.14, f16[8,128,128]{2,1,0:T(8,128)(2,1)S(1)} %collective-permute-done.13, f16[8,128,128]{2,1,0:T(8,128)(2,1)S(1)} %collective-permute-done.8, f16[1,8,128,128]{3,2,1,0:T(8,128)(2,1)S(1)} %collective-permute-done.3, ...), kind=kLoop, calls=%fused_computation.55 | loop fusion | flops 5767168 | bytes 2359296 | tf_op jit(solution)/shard_map/convert_element_type | solution.py:114
  49.7 18.7 %all_to_all.5 = f16[8,128,128]{2,1,0:T(8,128)(2,1)S(1)} all-to-all(f16[8,128,128]{2,1,0:T(8,128)(2,1)S(1)} %multiply_convert_fusion.3), channel_id=1, replica_groups=mesh['x'=4,'ylo'=2,'yhi'=2,'z'=8,'core'=2] {'z'}, dimensions={0} | all-to-all | bytes 524288 | tf_op jit(solution)/shard_map/all_to_all | solution.py:154
  68.4 0.3 fusion.18
  68.7 0.0 copy-done
  68.7 0.0 copy-done.1
  68.7 0.0 copy-done.2
  68.7 0.7 %multiply_subtract_fusion = (f32[16384]{0:T(1024)}, f32[16384]{0:T(1024)}, f32[16384]{0:T(1024)}) fusion(f32[16384]{0:T(1024)S(1)} %copy-done, f32[128,128]{1,0:T(8,128)S(1)} %fusion.18, f32[16384]{0:T(1024)S(1)} %copy-done.1, f32[16384]{0:T(1024)S(1)} %copy-done.2), kind=kLoop, calls=%fused_computation.74 | loop fusion | flops 212992 | bytes 458752 | tf_op jit(solution)/shard_map/sub | solution.py:161
Async XLA Ops:
  4.5 11.2 %collective-permute-start.9 = (bf16[4,2,8,128,128]{4,3,2,1,0:T(8,128)(2,1)S(1)}, bf16[4,2,8,128,128]{4,3,2,1,0:T(8,128)(2,1)S(1)}, u32[]{:S(2)}, u32[]{:S(2)}) collective-permute-start(bf16[4,2,8,128,128]{4,3,2,1,0:T(8,128)(2,1)S(1)} %get-tuple-element.24), channel_id=1, source_target_pairs={{0,1},{1,0},{2,3},{3,2},{4,5},{5,4},{6,7},{7,6},{8,9},{9,8},{10,11... | collective-permute-start | bytes 6291464 | tf_op jit(solution)/shard_map/ppermute | solution.py:127
  7.0 3.2 %collective-permute-start.4 = (bf16[4,1,8,128,128]{4,3,2,1,0:T(8,128)(2,1)S(1)}, bf16[4,1,8,128,128]{4,3,2,1,0:T(8,128)(2,1)S(1)}, u32[]{:S(2)}, u32[]{:S(2)}) collective-permute-start(bf16[4,1,8,128,128]{4,3,2,1,0:T(8,128)(2,1)S(1)} %get-tuple-element.22), channel_id=1, source_target_pairs={{0,1},{1,0},{2,3},{3,2},{4,5},{5,4},{6,7},{7,6},{8,9},{9,8},{10,11... | collective-permute-start | bytes 3145736 | tf_op jit(solution)/shard_map/ppermute | solution.py:127
  9.9 7.8 %collective-permute-start = (bf16[4,1,8,128,128]{4,3,2,1,0:T(8,128)(2,1)S(1)}, bf16[4,1,8,128,128]{4,3,2,1,0:T(8,128)(2,1)S(1)}, u32[]{:S(2)}, u32[]{:S(2)}) collective-permute-start(bf16[4,1,8,128,128]{4,3,2,1,0:T(8,128)(2,1)S(1)} %get-tuple-element.20), channel_id=1, source_target_pairs={{0,1},{1,0},{2,3},{3,2},{4,5},{5,4},{6,7},{7,6},{8,9},{9,8},{10,11... | collective-permute-start | bytes 3145736 | tf_op jit(solution)/shard_map/ppermute | solution.py:127
  10.6 8.1 %collective-permute-start.7 = (f16[1,8,128,128]{3,2,1,0:T(8,128)(2,1)S(1)}, f16[1,8,128,128]{3,2,1,0:T(8,128)(2,1)S(1)}, u32[]{:S(2)}, u32[]{:S(2)}) collective-permute-start(f16[1,8,128,128]{3,2,1,0:T(8,128)(2,1)S(1)} %get-tuple-element.35), channel_id=1, source_target_pairs={{0,192},{1,49},{2,194},{3,51},{4,196},{5,53},{6,198},{7,55},{8,200... | collective-permute-start | bytes 786440 | tf_op jit(solution)/shard_map/ppermute | solution.py:135
  13.4 10.4 %collective-permute-start.6 = (f16[1,8,128,128]{3,2,1,0:T(8,128)(2,1)S(1)}, f16[1,8,128,128]{3,2,1,0:T(8,128)(2,1)S(1)}, u32[]{:S(2)}, u32[]{:S(2)}) collective-permute-start(f16[1,8,128,128]{3,2,1,0:T(8,128)(2,1)S(1)} %get-tuple-element.36), channel_id=1, source_target_pairs={{0,64},{1,33},{2,66},{3,35},{4,68},{5,37},{6,70},{7,39},{8,72},{9,... | collective-permute-start | bytes 786440 | tf_op jit(solution)/shard_map/ppermute | solution.py:135
  13.4 10.4 %collective-permute-start.5 = (f16[1,8,128,128]{3,2,1,0:T(8,128)(2,1)S(1)}, f16[1,8,128,128]{3,2,1,0:T(8,128)(2,1)S(1)}, u32[]{:S(2)}, u32[]{:S(2)}) collective-permute-start(f16[1,8,128,128]{3,2,1,0:T(8,128)(2,1)S(1)} %get-tuple-element.34), channel_id=1, source_target_pairs={{0,128},{1,17},{2,130},{3,19},{4,132},{5,21},{6,134},{7,23},{8,136... | collective-permute-start | bytes 786440 | tf_op jit(solution)/shard_map/ppermute | solution.py:135
  16.5 11.0 %collective-permute-start.12 = (f16[2,8,128,128]{3,2,1,0:T(8,128)(2,1)S(1)}, f16[2,8,128,128]{3,2,1,0:T(8,128)(2,1)S(1)}, u32[]{:S(2)}, u32[]{:S(2)}) collective-permute-start(f16[2,8,128,128]{3,2,1,0:T(8,128)(2,1)S(1)} %get-tuple-element.29), channel_id=1, source_target_pairs={{0,192},{1,49},{2,194},{3,51},{4,196},{5,53},{6,198},{7,55},{8,200... | collective-permute-start | bytes 1572872 | tf_op jit(solution)/shard_map/ppermute | solution.py:135
  17.8 20.1 %collective-permute-start.11 = (f16[2,8,128,128]{3,2,1,0:T(8,128)(2,1)S(1)}, f16[2,8,128,128]{3,2,1,0:T(8,128)(2,1)S(1)}, u32[]{:S(2)}, u32[]{:S(2)}) collective-permute-start(f16[2,8,128,128]{3,2,1,0:T(8,128)(2,1)S(1)} %get-tuple-element.30), channel_id=1, source_target_pairs={{0,64},{1,33},{2,66},{3,35},{4,68},{5,37},{6,70},{7,39},{8,72},{9,... | collective-permute-start | bytes 1572872 | tf_op jit(solution)/shard_map/ppermute | solution.py:135
  18.6 19.2 %collective-permute-start.10 = (f16[2,8,128,128]{3,2,1,0:T(8,128)(2,1)S(1)}, f16[2,8,128,128]{3,2,1,0:T(8,128)(2,1)S(1)}, u32[]{:S(2)}, u32[]{:S(2)}) collective-permute-start(f16[2,8,128,128]{3,2,1,0:T(8,128)(2,1)S(1)} %get-tuple-element.28), channel_id=1, source_target_pairs={{0,128},{1,17},{2,130},{3,19},{4,132},{5,21},{6,134},{7,23},{8,136... | collective-permute-start | bytes 1572872 | tf_op jit(solution)/shard_map/ppermute | solution.py:135
  23.8 17.2 %collective-permute-start.3 = (f16[1,8,128,128]{3,2,1,0:T(8,128)(2,1)S(1)}, f16[1,8,128,128]{3,2,1,0:T(8,128)(2,1)S(1)}, u32[]{:S(2)}, u32[]{:S(2)}) collective-permute-start(f16[1,8,128,128]{3,2,1,0:T(8,128)(2,1)S(1)} %get-tuple-element.32), channel_id=1, source_target_pairs={{0,192},{1,49},{2,194},{3,51},{4,196},{5,53},{6,198},{7,55},{8,200... | collective-permute-start | bytes 786440 | tf_op jit(solution)/shard_map/ppermute | solution.py:135
  23.8 19.5 %collective-permute-start.2 = (f16[1,8,128,128]{3,2,1,0:T(8,128)(2,1)S(1)}, f16[1,8,128,128]{3,2,1,0:T(8,128)(2,1)S(1)}, u32[]{:S(2)}, u32[]{:S(2)}) collective-permute-start(f16[1,8,128,128]{3,2,1,0:T(8,128)(2,1)S(1)} %get-tuple-element.33), channel_id=1, source_target_pairs={{0,64},{1,33},{2,66},{3,35},{4,68},{5,37},{6,70},{7,39},{8,72},{9,... | collective-permute-start | bytes 786440 | tf_op jit(solution)/shard_map/ppermute | solution.py:135
  27.5 18.0 %collective-permute-start.1 = (f16[1,8,128,128]{3,2,1,0:T(8,128)(2,1)S(1)}, f16[1,8,128,128]{3,2,1,0:T(8,128)(2,1)S(1)}, u32[]{:S(2)}, u32[]{:S(2)}) collective-permute-start(f16[1,8,128,128]{3,2,1,0:T(8,128)(2,1)S(1)} %get-tuple-element.31), channel_id=1, source_target_pairs={{0,128},{1,17},{2,130},{3,19},{4,132},{5,21},{6,134},{7,23},{8,136... | collective-permute-start | bytes 786440 | tf_op jit(solution)/shard_map/ppermute | solution.py:135
  37.8 8.0 %collective-permute-start.8 = (f16[8,128,128]{2,1,0:T(8,128)(2,1)S(1)}, f16[8,128,128]{2,1,0:T(8,128)(2,1)S(1)}, u32[]{:S(2)}, u32[]{:S(2)}) collective-permute-start(f16[8,128,128]{2,1,0:T(8,128)(2,1)S(1)} %fusion.24), channel_id=1, source_target_pairs={{0,16},{1,129},{2,18},{3,131},{4,20},{5,133},{6,22},{7,135},{8,24}... | collective-permute-start | bytes 786440 | tf_op jit(solution)/shard_map/ppermute | solution.py:152
  38.3 30.4 %copy-start = (f32[16384]{0:T(1024)S(1)}, f32[16384]{0:T(1024)}, u32[]{:S(2)}) copy-start(f32[16384]{0:T(1024)} %param.5) | copy-start | bytes 196612
  38.3 30.4 %copy-start.1 = (f32[16384]{0:T(1024)S(1)}, f32[16384]{0:T(1024)}, u32[]{:S(2)}) copy-start(f32[16384]{0:T(1024)} %param.6) | copy-start | bytes 196612
  38.3 30.4 %copy-start.2 = (f32[16384]{0:T(1024)S(1)}, f32[16384]{0:T(1024)}, u32[]{:S(2)}) copy-start(f32[16384]{0:T(1024)} %param.7) | copy-start | bytes 196612
  38.6 8.7 %collective-permute-start.14 = (f16[8,128,128]{2,1,0:T(8,128)(2,1)S(1)}, f16[8,128,128]{2,1,0:T(8,128)(2,1)S(1)}, u32[]{:S(2)}, u32[]{:S(2)}) collective-permute-start(f16[8,128,128]{2,1,0:T(8,128)(2,1)S(1)} %get-tuple-element.38), channel_id=1, source_target_pairs={{0,48},{1,193},{2,50},{3,195},{4,52},{5,197},{6,54},{7,199},{8,56}... | collective-permute-start | bytes 786440 | tf_op jit(solution)/shard_map/ppermute | solution.py:152
  41.0 7.5 %collective-permute-start.13 = (f16[8,128,128]{2,1,0:T(8,128)(2,1)S(1)}, f16[8,128,128]{2,1,0:T(8,128)(2,1)S(1)}, u32[]{:S(2)}, u32[]{:S(2)}) collective-permute-start(f16[8,128,128]{2,1,0:T(8,128)(2,1)S(1)} %get-tuple-element.37), channel_id=1, source_target_pairs={{0,32},{1,65},{2,34},{3,67},{4,36},{5,69},{6,38},{7,71},{8,40},{9,... | collective-permute-start | bytes 786440 | tf_op jit(solution)/shard_map/ppermute | solution.py:152

commit v4 on v3

--- a/solution.py
+++ b/solution.py
@@ -151,6 +151,8 @@
         total = total + decode(
             lax.ppermute(encode(parts[k], 8), AXES, permutation(k, 1)), 8
         )
+        if k == 2:
+            total = lax.optimization_barrier(total)
     arrived = lax.all_to_all(
         encode(total, 32), "z", split_axis=0, concat_axis=0, tiled=True
     )

time: 70.1 us -> 69.7 us (level)
  no operation moved by 1% of the time
where the time goes in v4:
time: 69.7 us; the launch traced here: 68.9 us
  waiting for transfers between devices  23 us (33%)
  blocking collectives  18.7 us (27%)
  starting transfers between devices  13.3 us (19%)
  Pallas kernels  8.62 us (12%)
  other arithmetic  4.61 us (7%)
  between operations  0.74 us (1%)
    ppermute x9, waiting for transfers between devices, first_stage(): lax.ppermute(encode_pair(pair(k)), AXES, permutation(k, 0))  20.3 us
    all_to_all x1, blocking collectives, per_device(): lax.all_to_all(encode(total, 32), 'z', split_axis=0, concat_axis=0, tiled...  18.7 us
    ppermute x9, starting transfers between devices, first_stage(): lax.ppermute(encode_pair(pair(k)), AXES, permutation(k, 0))  12.2 us
    pallas_call x3, Pallas kernels, repack(): pl.pallas_call(functools.partial(repack_kernel, chunk), out_shape=(shape,...  8.62 us
    ppermute x3, waiting for transfers between devices, per_device(): lax.ppermute(encode(parts[k], 8), AXES, permutation(k, 1))  2.52 us
    convert_element_type x3, other arithmetic, encode_pair(): return (value * 1024.0).astype(jnp.float16)  1.47 us
  transfers between devices with their start and end apart: 15, of which 10 were waited for; matrix products, arithmetic and copies ran while one was open for 4% of the time, Pallas kernels for 7%

profile of v4, /device:TPU:16, one launch (start us, length us, event | category | flops | bytes accessed | tf_op | source)
XLA Modules:
  0.0 68.9 jit_solution(15162726622021191653)
XLA Ops:
  0.6 3.8 %shard_map.67 = (bf16[4,2,8,128,128]{4,3,2,1,0:T(8,128)(2,1)S(1)}, bf16[4,2,8,128,128]{4,3,2,1,0:T(8,128)(2,1)S(1)}) custom-call(bf16[1,4194304]{1,0:T(2,128)(2,1)} %grads.3), custom_call_target="tpu_custom_call" | custom-call | bytes 12582912 | tf_op jit(solution)/shard_map/pallas_call | solution.py:83
  4.5 0.1 collective-permute-start.9
  4.6 2.4 %shard_map.68 = (bf16[4,1,8,128,128]{4,3,2,1,0:T(8,128)(2,1)S(1)}, bf16[4,1,8,128,128]{4,3,2,1,0:T(8,128)(2,1)S(1)}) custom-call(bf16[1,4194304]{1,0:T(2,128)(2,1)} %grads.3), custom_call_target="tpu_custom_call" | custom-call | bytes 6291456 | tf_op jit(solution)/shard_map/pallas_call | solution.py:83
  7.0 0.5 collective-permute-start.4
  7.5 2.4 %shard_map.69 = (bf16[4,1,8,128,128]{4,3,2,1,0:T(8,128)(2,1)S(1)}, bf16[4,1,8,128,128]{4,3,2,1,0:T(8,128)(2,1)S(1)}) custom-call(bf16[1,4194304]{1,0:T(2,128)(2,1)} %grads.3), custom_call_target="tpu_custom_call" | custom-call | bytes 6291456 | tf_op jit(solution)/shard_map/pallas_call | solution.py:83
  9.9 0.1 collective-permute-start
  10.1 0.2 collective-permute-done.4
  10.2 0.3 fusion.32
  10.6 2.8 %collective-permute-start.7 = (f16[1,8,128,128]{3,2,1,0:T(8,128)(2,1)S(1)}, f16[1,8,128,128]{3,2,1,0:T(8,128)(2,1)S(1)}, u32[]{:S(2)}, u32[]{:S(2)}) collective-permute-start(f16[1,8,128,128]{3,2,1,0:T(8,128)(2,1)S(1)} %get-tuple-element.35), channel_id=1, source_target_pairs={{0,192},{1,49},{2,194},{3,51},{4,196},{5,53},{6,198},{7,55},{8,200... | collective-permute-start | bytes 786440 | tf_op jit(solution)/shard_map/ppermute | solution.py:135
  13.4 0.0 collective-permute-start.6
  13.4 2.3 %collective-permute-start.5 = (f16[1,8,128,128]{3,2,1,0:T(8,128)(2,1)S(1)}, f16[1,8,128,128]{3,2,1,0:T(8,128)(2,1)S(1)}, u32[]{:S(2)}, u32[]{:S(2)}) collective-permute-start(f16[1,8,128,128]{3,2,1,0:T(8,128)(2,1)S(1)} %get-tuple-element.34), channel_id=1, source_target_pairs={{0,128},{1,17},{2,130},{3,19},{4,132},{5,21},{6,134},{7,23},{8,136... | collective-permute-start | bytes 786440 | tf_op jit(solution)/shard_map/ppermute | solution.py:135
  15.7 0.0 collective-permute-done.9
  15.7 0.8 %fusion.19 = (f16[2,8,128,128]{3,2,1,0:T(8,128)(2,1)S(1)}, f16[2,8,128,128]{3,2,1,0:T(8,128)(2,1)S(1)}, f16[2,8,128,128]{3,2,1,0:T(8,128)(2,1)S(1)}) fusion(bf16[4,2,8,128,128]{4,3,2,1,0:T(8,128)(2,1)S(1)} %collective-permute-done.9, bf16[4,2,8,128,128]{4,3,2,1,0:T(8,128)(2,1)S(1)} %get-tuple-element.23), kind=kLoop, calls=%fused_computation.39 | loop fusion | flops 3932160 | bytes 4718592 | tf_op jit(solution)/shard_map/convert_element_type | solution.py:100
  16.5 1.2 %collective-permute-start.12 = (f16[2,8,128,128]{3,2,1,0:T(8,128)(2,1)S(1)}, f16[2,8,128,128]{3,2,1,0:T(8,128)(2,1)S(1)}, u32[]{:S(2)}, u32[]{:S(2)}) collective-permute-start(f16[2,8,128,128]{3,2,1,0:T(8,128)(2,1)S(1)} %get-tuple-element.29), channel_id=1, source_target_pairs={{0,192},{1,49},{2,194},{3,51},{4,196},{5,53},{6,198},{7,55},{8,200... | collective-permute-start | bytes 1572872 | tf_op jit(solution)/shard_map/ppermute | solution.py:135
  17.8 0.0 collective-permute-done
  17.8 0.9 %collective-permute-start.11 = (f16[2,8,128,128]{3,2,1,0:T(8,128)(2,1)S(1)}, f16[2,8,128,128]{3,2,1,0:T(8,128)(2,1)S(1)}, u32[]{:S(2)}, u32[]{:S(2)}) collective-permute-start(f16[2,8,128,128]{3,2,1,0:T(8,128)(2,1)S(1)} %get-tuple-element.30), channel_id=1, source_target_pairs={{0,64},{1,33},{2,66},{3,35},{4,68},{5,37},{6,70},{7,39},{8,72},{9,... | collective-permute-start | bytes 1572872 | tf_op jit(solution)/shard_map/ppermute | solution.py:135
  18.6 0.0 collective-permute-done.7
  18.6 1.9 %collective-permute-start.10 = (f16[2,8,128,128]{3,2,1,0:T(8,128)(2,1)S(1)}, f16[2,8,128,128]{3,2,1,0:T(8,128)(2,1)S(1)}, u32[]{:S(2)}, u32[]{:S(2)}) collective-permute-start(f16[2,8,128,128]{3,2,1,0:T(8,128)(2,1)S(1)} %get-tuple-element.28), channel_id=1, source_target_pairs={{0,128},{1,17},{2,130},{3,19},{4,132},{5,21},{6,134},{7,23},{8,136... | collective-permute-start | bytes 1572872 | tf_op jit(solution)/shard_map/ppermute | solution.py:135
  20.6 0.3 fusion.29
  20.9 2.9 %collective-permute-done.6 = f16[1,8,128,128]{3,2,1,0:T(8,128)(2,1)S(1)} collective-permute-done((f16[1,8,128,128]{3,2,1,0:T(8,128)(2,1)S(1)}, f16[1,8,128,128]{3,2,1,0:T(8,128)(2,1)S(1)}, u32[]{:S(2)}, u32[]{:S(2)}) %collective-permute-start.6) | collective-permute-done | bytes 262176 | tf_op jit(solution)/shard_map/ppermute | solution.py:135
  23.8 0.0 collective-permute-start.3
  23.8 0.0 collective-permute-done.5
  23.8 2.0 %collective-permute-start.2 = (f16[1,8,128,128]{3,2,1,0:T(8,128)(2,1)S(1)}, f16[1,8,128,128]{3,2,1,0:T(8,128)(2,1)S(1)}, u32[]{:S(2)}, u32[]{:S(2)}) collective-permute-start(f16[1,8,128,128]{3,2,1,0:T(8,128)(2,1)S(1)} %get-tuple-element.33), channel_id=1, source_target_pairs={{0,64},{1,33},{2,66},{3,35},{4,68},{5,37},{6,70},{7,39},{8,72},{9,... | collective-permute-start | bytes 786440 | tf_op jit(solution)/shard_map/ppermute | solution.py:135
  25.8 0.3 fusion.24
  26.1 1.4 %collective-permute-done.12 = f16[2,8,128,128]{3,2,1,0:T(8,128)(2,1)S(1)} collective-permute-done((f16[2,8,128,128]{3,2,1,0:T(8,128)(2,1)S(1)}, f16[2,8,128,128]{3,2,1,0:T(8,128)(2,1)S(1)}, u32[]{:S(2)}, u32[]{:S(2)}) %collective-permute-start.12) | collective-permute-done | bytes 524320 | tf_op jit(solution)/shard_map/ppermute | solution.py:135
  27.5 1.0 %collective-permute-start.1 = (f16[1,8,128,128]{3,2,1,0:T(8,128)(2,1)S(1)}, f16[1,8,128,128]{3,2,1,0:T(8,128)(2,1)S(1)}, u32[]{:S(2)}, u32[]{:S(2)}) collective-permute-start(f16[1,8,128,128]{3,2,1,0:T(8,128)(2,1)S(1)} %get-tuple-element.31), channel_id=1, source_target_pairs={{0,128},{1,17},{2,130},{3,19},{4,132},{5,21},{6,134},{7,23},{8,136... | collective-permute-start | bytes 786440 | tf_op jit(solution)/shard_map/ppermute | solution.py:135
  28.5 9.4 %collective-permute-done.11 = f16[2,8,128,128]{3,2,1,0:T(8,128)(2,1)S(1)} collective-permute-done((f16[2,8,128,128]{3,2,1,0:T(8,128)(2,1)S(1)}, f16[2,8,128,128]{3,2,1,0:T(8,128)(2,1)S(1)}, u32[]{:S(2)}, u32[]{:S(2)}) %collective-permute-start.11) | collective-permute-done | bytes 524320 | tf_op jit(solution)/shard_map/ppermute | solution.py:135
  37.8 0.0 collective-permute-start.8
  37.8 0.0 collective-permute-done.10
  37.8 0.5 fusion.1
  38.3 0.2 multiply_convert_fusion.5
  38.6 0.3 collective-permute-start.14
  38.8 2.2 %collective-permute-done.3 = f16[1,8,128,128]{3,2,1,0:T(8,128)(2,1)S(1)} collective-permute-done((f16[1,8,128,128]{3,2,1,0:T(8,128)(2,1)S(1)}, f16[1,8,128,128]{3,2,1,0:T(8,128)(2,1)S(1)}, u32[]{:S(2)}, u32[]{:S(2)}) %collective-permute-start.3) | collective-permute-done | bytes 262176 | tf_op jit(solution)/shard_map/ppermute | solution.py:135
  41.0 0.0 copy-start
  41.0 0.0 copy-start.1
  41.0 0.0 copy-start.2
  41.0 0.0 collective-permute-start.13
  41.1 2.1 %collective-permute-done.2 = f16[1,8,128,128]{3,2,1,0:T(8,128)(2,1)S(1)} collective-permute-done((f16[1,8,128,128]{3,2,1,0:T(8,128)(2,1)S(1)}, f16[1,8,128,128]{3,2,1,0:T(8,128)(2,1)S(1)}, u32[]{:S(2)}, u32[]{:S(2)}) %collective-permute-start.2) | collective-permute-done | bytes 262176 | tf_op jit(solution)/shard_map/ppermute | solution.py:135
  43.2 2.3 %collective-permute-done.1 = f16[1,8,128,128]{3,2,1,0:T(8,128)(2,1)S(1)} collective-permute-done((f16[1,8,128,128]{3,2,1,0:T(8,128)(2,1)S(1)}, f16[1,8,128,128]{3,2,1,0:T(8,128)(2,1)S(1)}, u32[]{:S(2)}, u32[]{:S(2)}) %collective-permute-start.1) | collective-permute-done | bytes 262176 | tf_op jit(solution)/shard_map/ppermute | solution.py:135
  45.5 0.3 collective-permute-done.8
  45.8 0.5 fusion.14
  46.3 1.0 %collective-permute-done.14 = f16[8,128,128]{2,1,0:T(8,128)(2,1)S(1)} collective-permute-done((f16[8,128,128]{2,1,0:T(8,128)(2,1)S(1)}, f16[8,128,128]{2,1,0:T(8,128)(2,1)S(1)}, u32[]{:S(2)}, u32[]{:S(2)}) %collective-permute-start.14) | collective-permute-done | bytes 262176 | tf_op jit(solution)/shard_map/ppermute | solution.py:152
  47.3 1.2 %collective-permute-done.13 = f16[8,128,128]{2,1,0:T(8,128)(2,1)S(1)} collective-permute-done((f16[8,128,128]{2,1,0:T(8,128)(2,1)S(1)}, f16[8,128,128]{2,1,0:T(8,128)(2,1)S(1)}, u32[]{:S(2)}, u32[]{:S(2)}) %collective-permute-start.13) | collective-permute-done | bytes 262176 | tf_op jit(solution)/shard_map/ppermute | solution.py:152
  48.5 0.7 multiply_convert_fusion.3
  49.2 18.7 %all_to_all.5 = f16[8,128,128]{2,1,0:T(8,128)(2,1)S(1)} all-to-all(f16[8,128,128]{2,1,0:T(8,128)(2,1)S(1)} %multiply_convert_fusion.3), channel_id=1, replica_groups=mesh['x'=4,'ylo'=2,'yhi'=2,'z'=8,'core'=2] {'z'}, dimensions={0} | all-to-all | bytes 524288 | tf_op jit(solution)/shard_map/all_to_all | solution.py:156
  67.9 0.3 fusion.18
  68.2 0.0 copy-done
  68.2 0.0 copy-done.1
  68.2 0.0 copy-done.2
  68.3 0.7 %multiply_subtract_fusion = (f32[16384]{0:T(1024)}, f32[16384]{0:T(1024)}, f32[16384]{0:T(1024)}) fusion(f32[16384]{0:T(1024)S(1)} %copy-done, f32[128,128]{1,0:T(8,128)S(1)} %fusion.18, f32[16384]{0:T(1024)S(1)} %copy-done.1, f32[16384]{0:T(1024)S(1)} %copy-done.2), kind=kLoop, calls=%fused_computation.74 | loop fusion | flops 212992 | bytes 458752 | tf_op jit(solution)/shard_map/sub | solution.py:163
Async XLA Ops:
  4.5 11.2 %collective-permute-start.9 = (bf16[4,2,8,128,128]{4,3,2,1,0:T(8,128)(2,1)S(1)}, bf16[4,2,8,128,128]{4,3,2,1,0:T(8,128)(2,1)S(1)}, u32[]{:S(2)}, u32[]{:S(2)}) collective-permute-start(bf16[4,2,8,128,128]{4,3,2,1,0:T(8,128)(2,1)S(1)} %get-tuple-element.24), channel_id=1, source_target_pairs={{0,1},{1,0},{2,3},{3,2},{4,5},{5,4},{6,7},{7,6},{8,9},{9,8},{10,11... | collective-permute-start | bytes 6291464 | tf_op jit(solution)/shard_map/ppermute | solution.py:127
  7.0 3.2 %collective-permute-start.4 = (bf16[4,1,8,128,128]{4,3,2,1,0:T(8,128)(2,1)S(1)}, bf16[4,1,8,128,128]{4,3,2,1,0:T(8,128)(2,1)S(1)}, u32[]{:S(2)}, u32[]{:S(2)}) collective-permute-start(bf16[4,1,8,128,128]{4,3,2,1,0:T(8,128)(2,1)S(1)} %get-tuple-element.22), channel_id=1, source_target_pairs={{0,1},{1,0},{2,3},{3,2},{4,5},{5,4},{6,7},{7,6},{8,9},{9,8},{10,11... | collective-permute-start | bytes 3145736 | tf_op jit(solution)/shard_map/ppermute | solution.py:127
  9.9 7.8 %collective-permute-start = (bf16[4,1,8,128,128]{4,3,2,1,0:T(8,128)(2,1)S(1)}, bf16[4,1,8,128,128]{4,3,2,1,0:T(8,128)(2,1)S(1)}, u32[]{:S(2)}, u32[]{:S(2)}) collective-permute-start(bf16[4,1,8,128,128]{4,3,2,1,0:T(8,128)(2,1)S(1)} %get-tuple-element.20), channel_id=1, source_target_pairs={{0,1},{1,0},{2,3},{3,2},{4,5},{5,4},{6,7},{7,6},{8,9},{9,8},{10,11... | collective-permute-start | bytes 3145736 | tf_op jit(solution)/shard_map/ppermute | solution.py:127
  10.6 8.1 %collective-permute-start.7 = (f16[1,8,128,128]{3,2,1,0:T(8,128)(2,1)S(1)}, f16[1,8,128,128]{3,2,1,0:T(8,128)(2,1)S(1)}, u32[]{:S(2)}, u32[]{:S(2)}) collective-permute-start(f16[1,8,128,128]{3,2,1,0:T(8,128)(2,1)S(1)} %get-tuple-element.35), channel_id=1, source_target_pairs={{0,192},{1,49},{2,194},{3,51},{4,196},{5,53},{6,198},{7,55},{8,200... | collective-permute-start | bytes 786440 | tf_op jit(solution)/shard_map/ppermute | solution.py:135
  13.4 10.4 %collective-permute-start.6 = (f16[1,8,128,128]{3,2,1,0:T(8,128)(2,1)S(1)}, f16[1,8,128,128]{3,2,1,0:T(8,128)(2,1)S(1)}, u32[]{:S(2)}, u32[]{:S(2)}) collective-permute-start(f16[1,8,128,128]{3,2,1,0:T(8,128)(2,1)S(1)} %get-tuple-element.36), channel_id=1, source_target_pairs={{0,64},{1,33},{2,66},{3,35},{4,68},{5,37},{6,70},{7,39},{8,72},{9,... | collective-permute-start | bytes 786440 | tf_op jit(solution)/shard_map/ppermute | solution.py:135
  13.4 10.4 %collective-permute-start.5 = (f16[1,8,128,128]{3,2,1,0:T(8,128)(2,1)S(1)}, f16[1,8,128,128]{3,2,1,0:T(8,128)(2,1)S(1)}, u32[]{:S(2)}, u32[]{:S(2)}) collective-permute-start(f16[1,8,128,128]{3,2,1,0:T(8,128)(2,1)S(1)} %get-tuple-element.34), channel_id=1, source_target_pairs={{0,128},{1,17},{2,130},{3,19},{4,132},{5,21},{6,134},{7,23},{8,136... | collective-permute-start | bytes 786440 | tf_op jit(solution)/shard_map/ppermute | solution.py:135
  16.5 11.0 %collective-permute-start.12 = (f16[2,8,128,128]{3,2,1,0:T(8,128)(2,1)S(1)}, f16[2,8,128,128]{3,2,1,0:T(8,128)(2,1)S(1)}, u32[]{:S(2)}, u32[]{:S(2)}) collective-permute-start(f16[2,8,128,128]{3,2,1,0:T(8,128)(2,1)S(1)} %get-tuple-element.29), channel_id=1, source_target_pairs={{0,192},{1,49},{2,194},{3,51},{4,196},{5,53},{6,198},{7,55},{8,200... | collective-permute-start | bytes 1572872 | tf_op jit(solution)/shard_map/ppermute | solution.py:135
  17.8 20.1 %collective-permute-start.11 = (f16[2,8,128,128]{3,2,1,0:T(8,128)(2,1)S(1)}, f16[2,8,128,128]{3,2,1,0:T(8,128)(2,1)S(1)}, u32[]{:S(2)}, u32[]{:S(2)}) collective-permute-start(f16[2,8,128,128]{3,2,1,0:T(8,128)(2,1)S(1)} %get-tuple-element.30), channel_id=1, source_target_pairs={{0,64},{1,33},{2,66},{3,35},{4,68},{5,37},{6,70},{7,39},{8,72},{9,... | collective-permute-start | bytes 1572872 | tf_op jit(solution)/shard_map/ppermute | solution.py:135
  18.6 19.2 %collective-permute-start.10 = (f16[2,8,128,128]{3,2,1,0:T(8,128)(2,1)S(1)}, f16[2,8,128,128]{3,2,1,0:T(8,128)(2,1)S(1)}, u32[]{:S(2)}, u32[]{:S(2)}) collective-permute-start(f16[2,8,128,128]{3,2,1,0:T(8,128)(2,1)S(1)} %get-tuple-element.28), channel_id=1, source_target_pairs={{0,128},{1,17},{2,130},{3,19},{4,132},{5,21},{6,134},{7,23},{8,136... | collective-permute-start | bytes 1572872 | tf_op jit(solution)/shard_map/ppermute | solution.py:135
  23.8 17.2 %collective-permute-start.3 = (f16[1,8,128,128]{3,2,1,0:T(8,128)(2,1)S(1)}, f16[1,8,128,128]{3,2,1,0:T(8,128)(2,1)S(1)}, u32[]{:S(2)}, u32[]{:S(2)}) collective-permute-start(f16[1,8,128,128]{3,2,1,0:T(8,128)(2,1)S(1)} %get-tuple-element.32), channel_id=1, source_target_pairs={{0,192},{1,49},{2,194},{3,51},{4,196},{5,53},{6,198},{7,55},{8,200... | collective-permute-start | bytes 786440 | tf_op jit(solution)/shard_map/ppermute | solution.py:135
  23.8 19.4 %collective-permute-start.2 = (f16[1,8,128,128]{3,2,1,0:T(8,128)(2,1)S(1)}, f16[1,8,128,128]{3,2,1,0:T(8,128)(2,1)S(1)}, u32[]{:S(2)}, u32[]{:S(2)}) collective-permute-start(f16[1,8,128,128]{3,2,1,0:T(8,128)(2,1)S(1)} %get-tuple-element.33), channel_id=1, source_target_pairs={{0,64},{1,33},{2,66},{3,35},{4,68},{5,37},{6,70},{7,39},{8,72},{9,... | collective-permute-start | bytes 786440 | tf_op jit(solution)/shard_map/ppermute | solution.py:135
  27.5 18.0 %collective-permute-start.1 = (f16[1,8,128,128]{3,2,1,0:T(8,128)(2,1)S(1)}, f16[1,8,128,128]{3,2,1,0:T(8,128)(2,1)S(1)}, u32[]{:S(2)}, u32[]{:S(2)}) collective-permute-start(f16[1,8,128,128]{3,2,1,0:T(8,128)(2,1)S(1)} %get-tuple-element.31), channel_id=1, source_target_pairs={{0,128},{1,17},{2,130},{3,19},{4,132},{5,21},{6,134},{7,23},{8,136... | collective-permute-start | bytes 786440 | tf_op jit(solution)/shard_map/ppermute | solution.py:135
  37.8 8.0 %collective-permute-start.8 = (f16[8,128,128]{2,1,0:T(8,128)(2,1)S(1)}, f16[8,128,128]{2,1,0:T(8,128)(2,1)S(1)}, u32[]{:S(2)}, u32[]{:S(2)}) collective-permute-start(f16[8,128,128]{2,1,0:T(8,128)(2,1)S(1)} %fusion.24), channel_id=1, source_target_pairs={{0,16},{1,129},{2,18},{3,131},{4,20},{5,133},{6,22},{7,135},{8,24}... | collective-permute-start | bytes 786440 | tf_op jit(solution)/shard_map/ppermute | solution.py:152
  38.6 8.8 %collective-permute-start.14 = (f16[8,128,128]{2,1,0:T(8,128)(2,1)S(1)}, f16[8,128,128]{2,1,0:T(8,128)(2,1)S(1)}, u32[]{:S(2)}, u32[]{:S(2)}) collective-permute-start(f16[8,128,128]{2,1,0:T(8,128)(2,1)S(1)} %get-tuple-element.38), channel_id=1, source_target_pairs={{0,48},{1,193},{2,50},{3,195},{4,52},{5,197},{6,54},{7,199},{8,56}... | collective-permute-start | bytes 786440 | tf_op jit(solution)/shard_map/ppermute | solution.py:152
  41.0 27.2 %copy-start = (f32[16384]{0:T(1024)S(1)}, f32[16384]{0:T(1024)}, u32[]{:S(2)}) copy-start(f32[16384]{0:T(1024)} %param.5) | copy-start | bytes 196612
  41.0 27.2 %copy-start.1 = (f32[16384]{0:T(1024)S(1)}, f32[16384]{0:T(1024)}, u32[]{:S(2)}) copy-start(f32[16384]{0:T(1024)} %param.6) | copy-start | bytes 196612
  41.0 27.2 %copy-start.2 = (f32[16384]{0:T(1024)S(1)}, f32[16384]{0:T(1024)}, u32[]{:S(2)}) copy-start(f32[16384]{0:T(1024)} %param.7) | copy-start | bytes 196612
  41.0 7.5 %collective-permute-start.13 = (f16[8,128,128]{2,1,0:T(8,128)(2,1)S(1)}, f16[8,128,128]{2,1,0:T(8,128)(2,1)S(1)}, u32[]{:S(2)}, u32[]{:S(2)}) collective-permute-start(f16[8,128,128]{2,1,0:T(8,128)(2,1)S(1)} %get-tuple-element.37), channel_id=1, source_target_pairs={{0,32},{1,65},{2,34},{3,67},{4,36},{5,69},{6,38},{7,71},{8,40},{9,... | collective-permute-start | bytes 786440 | tf_op jit(solution)/shard_map/ppermute | solution.py:152
